TPU v7x, 32 devices: a whole 2x2x4 slice. The times are simulated.
32 devices in a mesh: replica: 4 (over y, core), fsdp: 8 (over z, x).
Axes of the slice: x: 2, y: 2, z: 4, core: 2. Of those that a mesh axis runs over, the one named last changes fastest.
Arguments:
- gradients: bfloat16 [4, 1024, 8192], P('replica', 'fsdp'), may hold values from -6 to 6
- left_factor: float32 [8, 2, 2, 512, 512], P('fsdp', None, None, 'replica'), may hold values from -6 to 6
- right_factor: float32 [8, 2, 2, 512, 512], P('fsdp', None, None, 'replica'), may hold values from -6 to 6
- left_root: bfloat16 [8, 2, 2, 512, 512], P('fsdp', None, None, 'replica'), may hold values from -0.25 to 0.25
- right_root: bfloat16 [8, 2, 2, 512, 512], P('fsdp'), may hold values from -0.25 to 0.25
- owner_table: int32 [2, 16], replicated, may hold values from 0 to 7, as said below
Outputs:
- left_next: float32 [8, 2, 2, 512, 512], P('fsdp', None, None, 'replica')
- right_next: float32 [8, 2, 2, 512, 512], P('fsdp', None, None, 'replica')
- update: bfloat16 [8, 2, 2, 512, 512], P('fsdp', None, None, 'replica')
Inputs may be any that keep to these rules, and one draw needn't show every extreme that they name: In each row of owner_table no owner is named more than 2 times.
All inputs are finite; a program needn't handle non-finite values.
Results may differ from a plain program's by a relative error of at most 0.02.
Values may be sent and summed in bfloat16 or wider, within the bound.
A program may use at most 64 MiB of HBM per device.

v0:
```python
import jax
import jax.numpy as jnp
from jax import lax
from jax.sharding import PartitionSpec as P

decay_rate = 0.9


def slot_table(owner_table, owner_count, slot_depth):
    block_cols = owner_table.shape[1]
    owner_match = (
        owner_table[:, :, None] == jnp.arange(owner_count, dtype=jnp.int32)[None, None, :]
    ).astype(jnp.int32)
    earlier = jnp.cumsum(owner_match, axis=1) - owner_match
    column_rank = jnp.sum(earlier * owner_match, axis=2)
    slot_match = (
        column_rank[:, :, None] == jnp.arange(slot_depth, dtype=jnp.int32)[None, None, :]
    ).astype(jnp.int32)
    joint = owner_match[:, :, None, :] * slot_match[:, :, :, None]
    column_ids = jnp.arange(block_cols, dtype=jnp.int32)[None, :, None, None]
    col_table = jnp.sum(joint * column_ids, axis=1)
    col_valid = jnp.sum(joint, axis=1)
    return (col_table, col_valid)


def shards(gradients, left_factor, right_factor, left_root, right_root, owner_table):
    local = gradients[0].astype(jnp.float32)
    row_count, col_count = local.shape
    fsdp_count = lax.axis_size("fsdp")
    block_size = left_factor.shape[-1]
    slot_depth = left_factor.shape[1]
    block_rows = left_factor.shape[2]
    share_rows = left_factor.shape[3]
    block_cols = col_count // block_size
    per_block = block_size // row_count
    summed = lax.psum(local.astype(jnp.bfloat16), "replica")
    col_table, col_valid = slot_table(owner_table, fsdp_count, slot_depth)
    owner_index = lax.axis_index("fsdp")
    replica_index = lax.axis_index("replica")
    my_row = owner_index // per_block
    column_pick = lax.dynamic_index_in_dim(col_table, my_row, 0, keepdims=False)
    slot_live = lax.dynamic_index_in_dim(col_valid, my_row, 0, keepdims=False)
    strip_rows = summed.shape[0]
    strips = jnp.transpose(summed.reshape(strip_rows, block_cols, block_size), (1, 0, 2))
    outgoing = jnp.take(strips, column_pick.reshape(-1), axis=0)
    outgoing = outgoing.reshape(slot_depth, fsdp_count, strip_rows, block_size)
    outgoing = outgoing * slot_live[:, :, None, None].astype(jnp.bfloat16)
    received = lax.all_to_all(outgoing, "fsdp", split_axis=1, concat_axis=1, tiled=True)
    whole_blocks = received.reshape(slot_depth, block_rows, block_size, block_size)
    scale = (1.0 - decay_rate) / block_size
    left_mine = left_factor[0]
    right_mine = right_factor[0]
    lroot_mine = left_root[0]
    rroot_mine = right_root[0]
    offset = replica_index * share_rows
    row_share = lax.dynamic_slice_in_dim(whole_blocks, offset, share_rows, 2)
    col_share = lax.dynamic_slice_in_dim(whole_blocks, offset, share_rows, 3)
    stat_left = jnp.einsum(
        "kjab,kjcb->kjac", row_share, whole_blocks, preferred_element_type=jnp.float32
    )
    stat_right = jnp.einsum(
        "kjba,kjbc->kjac", col_share, whole_blocks, preferred_element_type=jnp.float32
    )
    left_new = decay_rate * left_mine + scale * stat_left
    right_new = decay_rate * right_mine + scale * stat_right
    half = jnp.einsum(
        "kjab,kjbc->kjac", lroot_mine, whole_blocks, preferred_element_type=jnp.float32
    ).astype(jnp.bfloat16)
    result = jnp.einsum(
        "kjab,kjbc->kjac", half, rroot_mine, preferred_element_type=jnp.float32
    ).astype(jnp.bfloat16)
    return (left_new[None], right_new[None], result[None])


def solution(mesh):
    placed = (
        P("replica", "fsdp", None),
        P("fsdp", None, None, "replica", None),
        P("fsdp", None, None, "replica", None),
        P("fsdp", None, None, "replica", None),
        P("fsdp", None, None, None, None),
        P(),
    )
    return jax.shard_map(
        shards,
        mesh=mesh,
        in_specs=placed,
        out_specs=(
            P("fsdp", None, None, "replica", None),
            P("fsdp", None, None, "replica", None),
            P("fsdp", None, None, "replica", None),
        ),
        check_vma=False,
    )
```

profile of v0, /device:TPU:0, one launch (start us, length us, event | category | flops | bytes accessed | tf_op | source)
XLA Modules:
  0.0 146.3 jit_solution(10884678744896377388)
XLA Ops:
  7.2 0.0 copy-start
  7.2 0.0 all-reduce.2.cloned.1.call-start
  7.2 4.2 %copy.28 = bf16[1,128,8192]{1,2,0:T(8,128)(2,1)} copy(bf16[1,128,8192]{2,1,0:T(8,128)(2,1)} %param.6) | data formatting | bytes 4194304 | tf_op args[0]
  11.5 3.9 %copy.29 = bf16[128,16,512]{2,0,1:T(8,128)(2,1)} copy(bf16[128,16,512]{0,2,1:T(8,128)(2,1)} %bitcast.39) | data formatting | bytes 4194304 | tf_op jit(solution)/shard_map/reshape | solution.py:44
  15.4 0.0 all-reduce.2.cloned.1.call-update
  15.4 0.7 copy-done.5
  16.1 0.1 fusion.18
  16.2 0.1 copy.26
  16.3 0.2 select_reduce_fusion
  16.4 0.2 multiply_reduce_fusion
  16.7 0.1 reshape.81
  16.8 0.1 copy.27
  16.9 0.1 copy.31
  17.0 52.7 %all-reduce.2.cloned.1.call-done = bf16[16,128,512]{2,1,0:T(8,128)(2,1)} async-done(((bf16[16,128,512]{2,1,0:T(8,128)(2,1)}), bf16[16,128,512]{2,1,0:T(8,128)(2,1)}) %all-reduce.2.cloned.1.call-update) | async-done | bytes 2097168 | tf_op jit(solution)/shard_map/psum | solution.py:36
  69.7 3.6 %gather_fusion = bf16[16,128,512]{2,1,0:T(8,128)(2,1)} fusion(bf16[16,128,512]{2,1,0:T(8,128)(2,1)} %all-reduce.2.cloned.1.call-done, s32[1024]{0:T(1024)S(1)} %pad_clamp_fusion), kind=kCustom, calls=%fused_computation | custom fusion | bytes 4194368 | tf_op jit(solution)/shard_map/jit(_take)/gather | solution.py:45
  73.2 3.2 %fusion.2 = bf16[2,8,128,512]{3,2,0,1:T(8,128)(2,1)} fusion(bf16[2,8,128,512]{3,2,1,0:T(8,128)(2,1)} %bitcast.38, pred[2,8]{0,1:T(8,128)(4,1)S(1)} %copy.27, bf16[2,8]{0,1:T(8,128)(2,1)S(1)} %copy.31), kind=kLoop, calls=%fused_computation.4 | loop fusion | flops 2097152 | bytes 4194352 | tf_op jit(solution)/shard_map/mul | solution.py:47
  76.4 5.5 %all-to-all-start = ((bf16[2,8,128,512]{3,2,0,1:T(8,128)(2,1)}), bf16[2,8,128,512]{3,2,0,1:T(8,128)(2,1)}, u32[]{:S(2)}, u32[]{:S(2)}) async-start(bf16[2,8,128,512]{3,2,0,1:T(8,128)(2,1)} %fusion.2), calls=%async_computation | async-start | bytes 4194304 | tf_op jit(solution)/shard_map/all_to_all | solution.py:48
  81.9 48.3 %all-to-all-done = bf16[2,8,128,512]{3,2,0,1:T(8,128)(2,1)} async-done(((bf16[2,8,128,512]{3,2,0,1:T(8,128)(2,1)}), bf16[2,8,128,512]{3,2,0,1:T(8,128)(2,1)}, u32[]{:S(2)}, u32[]{:S(2)}) %all-to-all-start) | async-done | bytes 2097184 | tf_op jit(solution)/shard_map/all_to_all | solution.py:48
  130.2 1.8 %copy.32 = bf16[2,8,128,512]{3,2,1,0:T(8,128)(2,1)S(1)} copy(bf16[2,8,128,512]{3,2,0,1:T(8,128)(2,1)} %all-to-all-done) | data formatting | bytes 4194304 | tf_op jit(solution)/shard_map/all_to_all | solution.py:48
  132.0 1.5 %fusion.4 = f32[1,2,2,128,512]{4,3,2,1,0:T(8,128)} fusion(bf16[2,2,512,512]{3,2,1,0:T(8,128)(2,1)S(1)} %bitcast.34, f32[1,2,2,128,512]{4,3,2,1,0:T(8,128)S(1)} %copy-done.2, s32[]{:T(128)S(6)} %select_n.41), kind=kOutput, calls=%fused_computation.7 | convolution fusion | flops 269221888 | bytes 4718596 | tf_op jit(solution)/shard_map/kjba,kjbc->kjac/dot_general | solution.py:61
  133.5 0.2 copy-done.1
  133.7 0.4 copy-done.3
  134.1 1.8 %fusion.6 = f32[1,2,2,128,512]{4,3,2,1,0:T(8,128)} fusion(bf16[2,2,512,512]{3,2,1,0:T(8,128)(2,1)S(1)} %bitcast.35, f32[1,2,2,128,512]{4,3,2,1,0:T(8,128)S(1)} %copy-done.3, s32[]{:T(128)S(6)} %select_n.41), kind=kOutput, calls=%fused_computation.10 | convolution fusion | flops 269221888 | bytes 4718596 | tf_op jit(solution)/shard_map/kjab,kjcb->kjac/dot_general | solution.py:58
  135.9 3.6 %fusion.10 = bf16[1,2,2,128,512]{4,3,2,1,0:T(8,128)(2,1)} fusion(bf16[1,2,2,512,512]{4,3,2,1,0:T(8,128)(2,1)S(1)} %copy-done, bf16[2,2,512,512]{3,2,1,0:T(8,128)(2,1)} %bitcast.36, bf16[1,2,2,128,512]{4,3,2,1,0:T(8,128)(2,1)S(1)} %copy-done.4), kind=kOutput, calls=%fused_computation.13 | convolution fusion | flops 537395200 | bytes 5242880 | tf_op jit(solution)/shard_map/kjab,kjbc->kjac/dot_general | solution.py:69
  (14 shorter events, 0.1 us)
Async XLA Ops:
  7.2 128.7 %copy-start = (bf16[1,2,2,512,512]{4,3,2,1,0:T(8,128)(2,1)S(1)}, bf16[1,2,2,512,512]{4,3,2,1,0:T(8,128)(2,1)}, u32[]{:S(2)}) copy-start(bf16[1,2,2,512,512]{4,3,2,1,0:T(8,128)(2,1)} %param.10) | copy-start | bytes 6291460
  7.2 62.5 %all-reduce.2.cloned.1.call-start = ((), (), s32[]{:S(2)}) async-start(), calls=%async_computation.1 | async-start | bytes 4194304 | tf_op jit(solution)/shard_map/psum | solution.py:36
  15.4 0.7 copy-start.5
  76.4 53.8 %all-to-all-start = ((bf16[2,8,128,512]{3,2,0,1:T(8,128)(2,1)}), bf16[2,8,128,512]{3,2,0,1:T(8,128)(2,1)}, u32[]{:S(2)}, u32[]{:S(2)}) async-start(bf16[2,8,128,512]{3,2,0,1:T(8,128)(2,1)} %fusion.2), calls=%async_computation | async-start | bytes 4194304 | tf_op jit(solution)/shard_map/all_to_all | solution.py:48
  81.9 50.1 %copy-start.2 = (f32[1,2,2,128,512]{4,3,2,1,0:T(8,128)S(1)}, f32[1,2,2,128,512]{4,3,2,1,0:T(8,128)}, u32[]{:S(2)}) copy-start(f32[1,2,2,128,512]{4,3,2,1,0:T(8,128)} %param.8) | copy-start | bytes 3145732
  132.0 1.7 %copy-start.1 = (bf16[2,8,128,512]{3,2,1,0:T(8,128)(2,1)}, bf16[2,8,128,512]{3,2,1,0:T(8,128)(2,1)S(1)}, u32[]{:S(2)}) copy-start(bf16[2,8,128,512]{3,2,1,0:T(8,128)(2,1)S(1)} %copy.32) | copy-start | bytes 6291460
  132.0 2.0 %copy-start.3 = (f32[1,2,2,128,512]{4,3,2,1,0:T(8,128)S(1)}, f32[1,2,2,128,512]{4,3,2,1,0:T(8,128)}, u32[]{:S(2)}) copy-start(f32[1,2,2,128,512]{4,3,2,1,0:T(8,128)} %param.7) | copy-start | bytes 3145732
  134.1 1.8 %copy-start.4 = (bf16[1,2,2,128,512]{4,3,2,1,0:T(8,128)(2,1)S(1)}, bf16[1,2,2,128,512]{4,3,2,1,0:T(8,128)(2,1)}, u32[]{:S(2)}) copy-start(bf16[1,2,2,128,512]{4,3,2,1,0:T(8,128)(2,1)} %param.9) | copy-start | bytes 1572868
Sparse Core Ops, SparseCore 0:
  15.5 54.0 all-reduce.1
where the time goes:
time: 147 us; the launch traced here: 146 us
  waiting for transfers between devices  101 us (69%)
  local copies, waits for them, and re-layouts  15.1 us (10%)
  between operations  14.1 us (10%)
  matrix products  6.83 us (5%)
  starting transfers between devices  5.55 us (4%)
  other arithmetic  3.76 us (3%)
    psum x1, waiting for transfers between devices, shards(): summed = lax.psum(local.astype(jnp.bfloat16), 'replica')  52.7 us
    all_to_all x1, waiting for transfers between devices, shards(): lax.all_to_all(outgoing, 'fsdp', split_axis=1, concat_axis=1, tiled=True)  48.3 us
    all_to_all x1, starting transfers between devices, shards(): lax.all_to_all(outgoing, 'fsdp', split_axis=1, concat_axis=1, tiled=True)  5.51 us
    unnamed x13, local copies, waits for them, and re-layouts  5.45 us
    reshape x1, local copies, waits for them, and re-layouts, shards(): summed.reshape(strip_rows, block_cols, block_size)  3.93 us
    gather x1, local copies, waits for them, and re-layouts, shards(): outgoing = jnp.take(strips, column_pick.reshape(-1), axis=0)  3.56 us
    dot_general x1, matrix products, shards(): jnp.einsum('kjab,kjbc->kjac', half, rroot_mine, preferred_element_type=jn...  3.55 us
    mul x1, other arithmetic, shards(): outgoing = outgoing * slot_live[:, :, None, None].astype(jnp.bfloat16)  3.21 us
  transfers between devices with their start and end apart: 2, of which 2 were waited for; matrix products, arithmetic and copies ran while one was open for 1% of the time, Pallas kernels for 0%

commit v1 on v0

v1 whole, which is shorter than its diff:
```python
import functools

import jax
import jax.numpy as jnp
from jax import lax
from jax.experimental import pallas as pl
from jax.experimental.pallas import tpu as pltpu
from jax.sharding import PartitionSpec as P

decay_rate = 0.9
MESH = pl.DeviceIdType.MESH
CORES = 2
HALVES = 2


def exchange(geo, table, grad, out, strip, cols, live, pair_out, pair_in, near_out, near_in, ready, blocks,
             load_sem, s1, r1, s2, r2, s3, r3, s4, r4, s5, r5, out_sem):
    depth, owners, ways, piece, width, halves, per_block, columns = geo
    part = width // halves
    chunks = depth * halves
    f = lax.axis_index("fsdp")
    r = lax.axis_index("replica")
    c, y = lax.rem(r, CORES), lax.div(r, CORES)
    mate = y * CORES + (1 - c)

    loads = []
    for col in range(columns):
        load = pltpu.make_async_copy(grad.at[0, :, pl.ds(col * width, width)], strip.at[col], load_sem.at[col])
        load.start()
        loads.append(load)

    def far_y(step):
        return lax.rem(y + step, ways)

    def far_f(step):
        return lax.rem(f + step, owners)

    barrier = pltpu.get_barrier_semaphore()
    pl.semaphore_signal(barrier, inc=1, device_id={"replica": mate}, device_id_type=MESH)
    for step in range(1, ways):
        pl.semaphore_signal(barrier, inc=1, device_id={"replica": far_y(step) * CORES + c}, device_id_type=MESH)
    for step in range(1, owners):
        pl.semaphore_signal(barrier, inc=1, device_id={"fsdp": far_f(step)}, device_id_type=MESH)

    row = lax.div(f, per_block)

    def place(d, carry):
        seen = jnp.int32(0)
        spot = [jnp.int32(0)] * depth
        for col in range(columns):
            hit = table[row, col] == d
            for k in range(depth):
                spot[k] = jnp.where(hit & (seen == k), col, spot[k])
            seen = seen + hit.astype(jnp.int32)
        for k in range(depth):
            cols[k, d] = spot[k]
            live[k, d] = jnp.where(seen > k, 1, 0)
        return carry

    lax.fori_loop(0, owners, place, 0)
    pl.semaphore_wait(barrier, 1 + (ways - 1) + (owners - 1))
    for load in loads:
        load.wait()

    def mine(n, d, q, core):
        k, h = n // halves, n % halves
        top = pl.multiple_of((q * CORES + core) * piece, 16)
        return strip[cols[k, d], pl.ds(top, piece), h * part:(h + 1) * part]

    pending = []

    def send(src, dst, s, t, **to):
        copy = pltpu.make_async_remote_copy(
            src_ref=src, dst_ref=dst, send_sem=s, recv_sem=t, device_id=to, device_id_type=MESH
        )
        copy.start()
        pending.append(copy)
        return copy

    first = []
    for n in range(chunks):
        def fill(d, carry):
            for q in range(ways):
                pair_out[n, q, d] = mine(n, d, q, 1 - c)
            return carry

        lax.fori_loop(0, owners, fill, 0)
        first.append(send(pair_out.at[n], pair_in.at[n], s1.at[n], r1.at[n], replica=mate))

    second = []
    for n in range(chunks):
        first[n].wait_recv()
        sent = []
        for step in range(1, ways):
            q = far_y(step)

            def add(d, carry):
                total = mine(n, d, q, c).astype(jnp.float32) + pair_in[n, q, d].astype(jnp.float32)
                near_out[n, step, d] = total.astype(jnp.bfloat16)
                return carry

            lax.fori_loop(0, owners, add, 0)
            sent.append(send(near_out.at[n, step], near_in.at[n, step], s2.at[n, step], r2.at[n, step],
                             replica=q * CORES + c))
        second.append(sent)

    third = {}

    def to_owners(n):
        for copy in second[n]:
            copy.wait_recv()
        third[n] = []
        for step in range(owners):
            d = far_f(step)
            total = mine(n, d, y, c).astype(jnp.float32) + pair_in[n, y, d].astype(jnp.float32)
            for other in range(1, ways):
                total = total + near_in[n, other, d].astype(jnp.float32)
            total = (total * live[n // halves, d].astype(jnp.float32)).astype(jnp.bfloat16)
            if step == 0:
                blocks[n, f, r] = total
            else:
                ready[n, step] = total
                third[n].append(send(ready.at[n, step], blocks.at[n, f, r], s3.at[n, step], r3.at[n, step], fsdp=d))

    fourth = {}

    def to_near(n):
        for copy in third[n]:
            copy.wait_recv()
        fourth[n] = []
        for step in range(1, ways):
            fourth[n].append(send(blocks.at[n, :, r], blocks.at[n, :, r], s4.at[n, step], r4.at[n, step],
                                  replica=far_y(step) * CORES + c))
        fourth[n].append(send(blocks.at[n, :, r], blocks.at[n, :, r], s5.at[n, 0], r5.at[n, 0], replica=mate))

    stored = []

    def to_mate(n):
        last = [fourth[n][-1]]
        for step in range(1, ways):
            fourth[n][step - 1].wait_recv()
            source = lax.rem(y + ways - step, ways) * CORES + c
            last.append(send(blocks.at[n, :, source], blocks.at[n, :, source], s5.at[n, step], r5.at[n, step],
                             replica=mate))
        for copy in last:
            copy.wait_recv()
        keep = pltpu.make_async_copy(blocks.at[n], out.at[n], out_sem.at[n])
        keep.start()
        stored.append(keep)

    for n in range(chunks):
        to_owners(n)
        if n >= 2:
            to_near(n - 2)
    for n in range(max(chunks - 2, 0), chunks):
        to_near(n)
        if n >= 2:
            to_mate(n - 2)
    for n in range(max(chunks - 2, 0), chunks):
        to_mate(n)
    for copy in pending:
        copy.wait_send()
    for keep in stored:
        keep.wait()


def precondition(halves, share, whole, left, right, lroot, rroot, left_out, right_out, update_out):
    r = lax.axis_index("replica")
    size = whole.shape[3]
    part = whole.shape[4]
    scale = (1.0 - decay_rate) / size
    block = jnp.concatenate([whole[0, h, 0] for h in range(halves)], axis=1)
    top = pl.multiple_of(r * share, 16)
    rows = jnp.concatenate([whole[0, h, 0, pl.ds(top, share), :] for h in range(halves)], axis=1)
    lanes = max(share, 128)
    group, shares = lax.div(r, lanes // share), lanes // share
    per = part // lanes
    col_start = pl.multiple_of(lax.rem(group, per) * lanes, 128)
    columns = whole[0, lax.div(group, per), 0, :, pl.ds(col_start, lanes)]
    f32 = jnp.float32
    stat_left = lax.dot_general(rows, block, (((1,), (1,)), ((), ())), preferred_element_type=f32)
    left_out[0, 0] = decay_rate * left[0, 0] + scale * stat_left
    stat_right = lax.dot_general(columns, block, (((0,), (0,)), ((), ())), preferred_element_type=f32)
    mine = stat_right[:share]
    for i in range(1, shares):
        mine = jnp.where(lax.rem(r, shares) == i, stat_right[i * share:(i + 1) * share], mine)
    right_out[0, 0] = decay_rate * right[0, 0] + scale * mine
    half = jnp.dot(lroot[0, 0], block, preferred_element_type=f32).astype(jnp.bfloat16)
    update_out[0, 0] = jnp.dot(half, rroot[0, 0], preferred_element_type=f32).astype(jnp.bfloat16)


def shards(gradients, left_factor, right_factor, left_root, right_root, owner_table):
    owners = lax.axis_size("fsdp")
    replicas = lax.axis_size("replica")
    ways = replicas // CORES
    strip_rows, total_cols = gradients.shape[1:]
    width = left_factor.shape[-1]
    depth, block_rows, share = left_factor.shape[1:4]
    columns = total_cols // width
    per_block = width // strip_rows
    piece = strip_rows // replicas
    halves = HALVES
    part = width // halves
    chunks = depth * halves
    geo = (depth, owners, ways, piece, width, halves, per_block, columns)
    bf16 = jnp.bfloat16
    dma = pltpu.SemaphoreType.DMA
    gathered = pl.pallas_call(
        functools.partial(exchange, geo),
        out_shape=jax.ShapeDtypeStruct((chunks, owners, replicas, piece, part), bf16),
        in_specs=[pl.BlockSpec(memory_space=pltpu.SMEM), pl.BlockSpec(memory_space=pl.ANY)],
        out_specs=pl.BlockSpec(memory_space=pl.ANY),
        scratch_shapes=[
            pltpu.VMEM((columns, strip_rows, width), bf16),
            pltpu.SMEM((depth, owners), jnp.int32),
            pltpu.SMEM((depth, owners), jnp.int32),
            pltpu.VMEM((chunks, ways, owners, piece, part), bf16),
            pltpu.VMEM((chunks, ways, owners, piece, part), bf16),
            pltpu.VMEM((chunks, ways, owners, piece, part), bf16),
            pltpu.VMEM((chunks, ways, owners, piece, part), bf16),
            pltpu.VMEM((chunks, owners, piece, part), bf16),
            pltpu.VMEM((chunks, owners, replicas, piece, part), bf16),
            dma((columns,)),
            dma((chunks,)), dma((chunks,)),
            dma((chunks, ways)), dma((chunks, ways)),
            dma((chunks, owners)), dma((chunks, owners)),
            dma((chunks, ways)), dma((chunks, ways)),
            dma((chunks, ways)), dma((chunks, ways)),
            dma((chunks,)),
        ],
        compiler_params=pltpu.CompilerParams(
            collective_id=0, has_side_effects=True, vmem_limit_bytes=40 * 1024 * 1024
        ),
    )(owner_table, gradients)
    blocks = gathered.reshape(depth, halves, block_rows, width, part)

    def at(k, j):
        return (k, j, 0, 0)

    factor = pl.BlockSpec((1, 1, share, width), at)
    left_new, right_new, update = pl.pallas_call(
        functools.partial(precondition, halves, share),
        grid=(depth, block_rows),
        out_shape=(
            jax.ShapeDtypeStruct(left_factor.shape[1:], jnp.float32),
            jax.ShapeDtypeStruct(left_factor.shape[1:], jnp.float32),
            jax.ShapeDtypeStruct(left_factor.shape[1:], bf16),
        ),
        in_specs=[
            pl.BlockSpec((1, halves, 1, width, part), lambda k, j: (k, 0, j, 0, 0)),
            factor,
            factor,
            factor,
            pl.BlockSpec((1, 1, width, width), at),
        ],
        out_specs=(factor, factor, factor),
        compiler_params=pltpu.CompilerParams(vmem_limit_bytes=32 * 1024 * 1024),
    )(blocks, left_factor[0], right_factor[0], left_root[0], right_root[0])
    return (left_new[None], right_new[None], update[None])


def solution(mesh):
    placed = (
        P("replica", "fsdp", None),
        P("fsdp", None, None, "replica", None),
        P("fsdp", None, None, "replica", None),
        P("fsdp", None, None, "replica", None),
        P("fsdp", None, None, None, None),
        P(),
    )
    factors = P("fsdp", None, None, "replica", None)
    return jax.shard_map(
        shards,
        mesh=mesh,
        in_specs=placed,
        out_specs=(factors, factors, factors),
        check_vma=False,
    )
```

time: 147 us -> 42.9 us (0.29)
  waiting for transfers between devices: 101 us -> 0 us
  Pallas kernels: 0 us -> 38.7 us
  between operations: 14.1 us -> 0.68 us
  local copies, waits for them, and re-layouts: 15.1 us -> 3.31 us
  matrix products: 6.83 us -> 0 us
  starting transfers between devices: 5.55 us -> 0 us
  other arithmetic: 3.76 us -> 0 us
    psum x1 -> x0, waiting for transfers between devices: 52.7 us -> none  [shards(): summed = lax.psum(local.astype(jnp.bfloat16), 'replica')]
    all_to_all x1 -> x0, waiting for transfers between devices: 48.3 us -> none  [shards(): lax.all_to_all(outgoing, 'fsdp', split_axis=1, concat_axis=1, tiled=True)]
    pallas_call x0 -> x2, Pallas kernels: none -> 38.7 us  [the longest x1 35.2 us: shards(): pl.pallas_call(functools.partial(exchange, geo), out_shape=jax.ShapeDtype...]
    dot_general x3 -> x0, matrix products: 6.83 us -> none  [the longest x1 3.55 us: shards(): jnp.einsum('kjab,kjbc->kjac', half, rroot_mine, preferred_element_type=jn...]
    all_to_all x1 -> x0, starting transfers between devices: 5.51 us -> none  [shards(): lax.all_to_all(outgoing, 'fsdp', split_axis=1, concat_axis=1, tiled=True)]
    reshape x2 -> x0, local copies, waits for them, and re-layouts: 4.01 us -> none  [the longest x1 3.93 us: shards(): summed.reshape(strip_rows, block_cols, block_size)]
    gather x1 -> x0, local copies, waits for them, and re-layouts: 3.56 us -> none  [shards(): outgoing = jnp.take(strips, column_pick.reshape(-1), axis=0)]
    mul x1 -> x0, other arithmetic: 3.21 us -> none  [shards(): outgoing = outgoing * slot_live[:, :, None, None].astype(jnp.bfloat16)]
  transfers between devices with their start and end apart: 2 -> 0, of which waited for: 2 -> 0; matrix products, arithmetic and copies ran while one was open for 1% -> 0% of each run, Pallas kernels for 0% -> 0%
where the time goes in v1:
time: 42.9 us; the launch traced here: 42.7 us
  Pallas kernels  38.7 us (90%)
  local copies, waits for them, and re-layouts  3.31 us (8%)
  between operations  0.68 us (2%)
    pallas_call x1, Pallas kernels, shards(): pl.pallas_call(functools.partial(exchange, geo), out_shape=jax.ShapeDtype...  35.2 us
    pallas_call x1, Pallas kernels, shards(): pl.pallas_call(functools.partial(precondition, halves, share), grid=(dept...  3.47 us
    unnamed x12, local copies, waits for them, and re-layouts  3.31 us

profile of v1, /device:TPU:0, one launch (start us, length us, event | category | flops | bytes accessed | tf_op | source)
XLA Modules:
  0.0 42.7 jit_solution(14144458424823758027)
XLA Ops:
  0.6 0.0 copy-start
  0.6 1.6 %copy-done = bf16[1,128,8192]{2,1,0:T(8,128)(2,1)S(1)} copy-done((bf16[1,128,8192]{2,1,0:T(8,128)(2,1)S(1)}, bf16[1,128,8192]{2,1,0:T(8,128)(2,1)}, u32[]{:S(2)}) %copy-start) | copy-done | bytes 2097176
  2.2 0.0 copy-start.5
  2.2 0.7 %copy-done.5 = s32[2,16]{1,0:T(2,128)S(1)} copy-done((s32[2,16]{1,0:T(2,128)S(1)}, s32[2,16]{1,0:T(2,128)}, u32[]{:S(2)}) %copy-start.5) | copy-done | bytes 152
  2.9 0.0 copy-start.1
  2.9 0.0 copy-start.2
  2.9 0.0 copy-start.3
  2.9 35.2 %shard_map.85 = bf16[4,8,4,32,256]{4,3,2,1,0:T(8,128)(2,1)S(1)} custom-call(s32[2,16]{1,0:T(2,128)S(1)} %copy-done.5, bf16[1,128,8192]{2,1,0:T(8,128)(2,1)S(1)} %copy-done), custom_call_target="tpu_custom_call" | custom-call | tf_op jit(solution)/shard_map/pallas_call | solution.py:208
  38.1 0.0 copy-done.1
  38.1 0.0 copy-done.2
  38.1 0.0 copy-done.3
  38.1 0.0 copy-start.4
  38.2 1.0 %copy-done.4 = bf16[1,2,2,128,512]{4,3,2,1,0:T(8,128)(2,1)S(1)} copy-done((bf16[1,2,2,128,512]{4,3,2,1,0:T(8,128)(2,1)S(1)}, bf16[1,2,2,128,512]{4,3,2,1,0:T(8,128)(2,1)}, u32[]{:S(2)}) %copy-start.4) | copy-done | bytes 524312
  39.2 3.5 %shard_map.86 = (f32[2,2,128,512]{3,2,1,0:T(8,128)}, f32[2,2,128,512]{3,2,1,0:T(8,128)}, bf16[2,2,128,512]{3,2,1,0:T(8,128)(2,1)}) custom-call(bf16[2,2,2,512,256]{4,3,2,1,0:T(8,128)(2,1)S(1)} %bitcast.8, f32[2,2,128,512]{3,2,1,0:T(8,128)S(1)} %bitcast.10, f32[2,2,128,512]{3,2,1,0:T(8,128)S(1)} %bitcast.11, bf16[2,2,128,512]{3,2,1,0:T(8,128)(2,1)S(1)} %bitcast.12, ...), custom_call_target="tpu_custom_call" | custom-call | tf_op jit(solution)/shard_map/pallas_call | solution.py:241
Async XLA Ops:
  0.6 1.6 %copy-start = (bf16[1,128,8192]{2,1,0:T(8,128)(2,1)S(1)}, bf16[1,128,8192]{2,1,0:T(8,128)(2,1)}, u32[]{:S(2)}) copy-start(bf16[1,128,8192]{2,1,0:T(8,128)(2,1)} %grad.1) | copy-start | bytes 6291460
  2.2 0.7 %copy-start.5 = (s32[2,16]{1,0:T(2,128)S(1)}, s32[2,16]{1,0:T(2,128)}, u32[]{:S(2)}) copy-start(s32[2,16]{1,0:T(2,128)} %table.1) | copy-start | bytes 388
  2.9 35.2 %copy-start.1 = (bf16[1,2,2,512,512]{4,3,2,1,0:T(8,128)(2,1)S(1)}, bf16[1,2,2,512,512]{4,3,2,1,0:T(8,128)(2,1)}, u32[]{:S(2)}) copy-start(bf16[1,2,2,512,512]{4,3,2,1,0:T(8,128)(2,1)} %param.10) | copy-start | bytes 6291460
  2.9 35.2 %copy-start.2 = (f32[1,2,2,128,512]{4,3,2,1,0:T(8,128)S(1)}, f32[1,2,2,128,512]{4,3,2,1,0:T(8,128)}, u32[]{:S(2)}) copy-start(f32[1,2,2,128,512]{4,3,2,1,0:T(8,128)} %param.7) | copy-start | bytes 3145732
  2.9 35.2 %copy-start.3 = (f32[1,2,2,128,512]{4,3,2,1,0:T(8,128)S(1)}, f32[1,2,2,128,512]{4,3,2,1,0:T(8,128)}, u32[]{:S(2)}) copy-start(f32[1,2,2,128,512]{4,3,2,1,0:T(8,128)} %param.8) | copy-start | bytes 3145732
  38.1 1.0 %copy-start.4 = (bf16[1,2,2,128,512]{4,3,2,1,0:T(8,128)(2,1)S(1)}, bf16[1,2,2,128,512]{4,3,2,1,0:T(8,128)(2,1)}, u32[]{:S(2)}) copy-start(bf16[1,2,2,128,512]{4,3,2,1,0:T(8,128)(2,1)} %param.9) | copy-start | bytes 1572868

commit v2 on v1

v2 whole, which is shorter than its diff:
```python
import functools
import math

import jax
import jax.numpy as jnp
from jax import lax
from jax.experimental import pallas as pl
from jax.experimental.pallas import tpu as pltpu
from jax.sharding import PartitionSpec as P

decay_rate = 0.9
MESH = pl.DeviceIdType.MESH
CORES = 2
SUB = 16


def exchange(geo, table, grad, out, owner_of, strip, other, same, cols, live, near_out, near_in, ready,
             table_sem, load_sem, s1, r1, s2, r2, s3, r3, s4, r4, s5, r5, own_sem):
    depth, owners, ways, piece, sub, width, per_block, columns = geo
    chunks = [(k, i) for k in range(depth) for i in range(piece // sub)]
    f = lax.axis_index("fsdp")
    r = lax.axis_index("replica")
    c, y = lax.rem(r, CORES), lax.div(r, CORES)
    mate = y * CORES + (1 - c)
    half = ways * piece

    def far_y(step):
        return lax.rem(y + step, ways)

    def far_f(step):
        return lax.rem(f + step, owners)

    barrier = pltpu.get_barrier_semaphore()
    pl.semaphore_signal(barrier, inc=1, device_id={"replica": mate}, device_id_type=MESH)
    for step in range(1, ways):
        pl.semaphore_signal(barrier, inc=1, device_id={"replica": far_y(step) * CORES + c}, device_id_type=MESH)
    for step in range(1, owners):
        pl.semaphore_signal(barrier, inc=1, device_id={"fsdp": far_f(step)}, device_id_type=MESH)
    names = pltpu.make_async_copy(table, owner_of, table_sem)
    names.start()
    top = pl.multiple_of(c * half, 16)
    for col in range(columns):
        pltpu.make_async_copy(
            grad.at[0, pl.ds(top, half), pl.ds(col * width, width)], strip.at[col], load_sem
        ).start()
    pl.semaphore_wait(barrier, 1 + (ways - 1) + (owners - 1))

    pending = []

    def copy_to(src, dst, s, t, **to):
        return pltpu.make_async_remote_copy(
            src_ref=src, dst_ref=dst, send_sem=s, recv_sem=t, device_id=to, device_id_type=MESH
        )

    def send(src, dst, s, t, **to):
        copy = copy_to(src, dst, s, t, **to)
        copy.start()
        pending.append(copy)
        return copy

    pairs = {}
    for step in list(range(1, ways)) + [0]:
        into = other.at[step - 1] if step else same
        start = pl.multiple_of((1 - c) * half + far_y(step) * piece, 16)
        for col in range(columns):
            copy_to(grad.at[0, pl.ds(start, piece), pl.ds(col * width, width)], into.at[col],
                    s1.at[step], r1.at[step], replica=mate).start()
        pairs[step] = copy_to(into, into, s1.at[step], r1.at[step], replica=mate)
        pending.append(pairs[step])

    names.wait()
    row = lax.div(f, per_block)

    def place(d, carry):
        seen = jnp.int32(0)
        spot = [jnp.int32(0)] * depth
        for col in range(columns):
            hit = owner_of[row, col] == d
            for k in range(depth):
                spot[k] = jnp.where(hit & (seen == k), col, spot[k])
            seen = seen + hit.astype(jnp.int32)
        for k in range(depth):
            cols[k, d] = spot[k]
            live[k, d] = jnp.where(seen > k, 1, 0)
        return carry

    lax.fori_loop(0, owners, place, 0)
    pltpu.make_async_copy(strip, strip, load_sem).wait()

    def pair(n, d, step, kind):
        k, i = chunks[n]
        col = cols[k, d]
        low = pl.multiple_of(far_y(step) * piece + i * sub, 16)
        here = pl.ds(i * sub, sub)
        theirs = other[step - 1, col, here, :] if step else same[col, here, :]
        return strip[col, pl.ds(low, sub), :].astype(kind) + theirs.astype(kind)

    second = [[] for _ in chunks]
    for step in range(1, ways):
        pairs[step].wait_recv()
    for n in range(len(chunks)):
        for step in range(1, ways):
            def add(d, carry):
                near_out[n, step - 1, d] = pair(n, d, step, jnp.bfloat16)
                return carry

            lax.fori_loop(0, owners, add, 0)
            second[n].append(send(near_out.at[n, step - 1], near_in.at[n, step - 1], s2.at[n, step], r2.at[n, step],
                                  replica=far_y(step) * CORES + c))
    pairs[0].wait_recv()

    def rows(n, source):
        k, i = chunks[n]
        spot = lax.rem(source, CORES) * ways + lax.div(source, CORES)
        return out.at[k, :, spot, pl.ds(i * sub, sub)]

    def row_of(n, source):
        k, i = chunks[n]
        spot = lax.rem(source, CORES) * ways + lax.div(source, CORES)
        return out.at[k, f, spot, pl.ds(i * sub, sub)]

    third = {}

    def to_owners(n):
        for copy in second[n]:
            copy.wait_recv()
        third[n] = []
        for step in list(range(1, owners)) + [0]:
            d = far_f(step)
            total = pair(n, d, 0, jnp.float32)
            for other_y in range(1, ways):
                total = total + near_in[n, other_y - 1, d].astype(jnp.float32)
            total = total * live[chunks[n][0], d].astype(jnp.float32)
            ready[n, step] = total.astype(jnp.bfloat16)
            if step == 0:
                own = pltpu.make_async_copy(ready.at[n, 0], row_of(n, r), own_sem.at[n])
                own.start()
                third[n].append(own)
            else:
                third[n].append(send(ready.at[n, step], row_of(n, r), s3.at[n, step], r3.at[n, step], fsdp=d))

    fourth = {}

    def to_near(n):
        third[n][-1].wait()
        for copy in third[n][:-1]:
            copy.wait_recv()
        fourth[n] = []
        for step in range(1, ways):
            fourth[n].append(send(rows(n, r), rows(n, r), s4.at[n, step], r4.at[n, step],
                                  replica=far_y(step) * CORES + c))
        fourth[n].append(send(rows(n, r), rows(n, r), s5.at[n, 0], r5.at[n, 0], replica=mate))

    last = []

    def to_mate(n):
        last.append(fourth[n][-1])
        for step in range(1, ways):
            fourth[n][step - 1].wait_recv()
            source = lax.rem(y + ways - step, ways) * CORES + c
            last.append(send(rows(n, source), rows(n, source), s5.at[n, step], r5.at[n, step], replica=mate))

    count = len(chunks)
    for n in range(count):
        to_owners(n)
        if n >= 2:
            to_near(n - 2)
    for n in range(max(count - 2, 0), count):
        to_near(n)
        if n >= 2:
            to_mate(n - 2)
    for n in range(max(count - 2, 0), count):
        to_mate(n)
    for copy in last:
        copy.wait_recv()
    for copy in pending:
        copy.wait_send()


def precondition(share, whole, left, right, lroot, rroot, left_out, right_out, update_out):
    r = lax.axis_index("replica")
    block = whole[0, 0]
    scale = (1.0 - decay_rate) / block.shape[0]
    rows = whole[0, 0, pl.ds(pl.multiple_of(r * share, 16), share), :]
    lanes = max(share, 128)
    shares = lanes // share
    columns = whole[0, 0, :, pl.ds(pl.multiple_of(lax.div(r, shares) * lanes, 128), lanes)]
    f32 = jnp.float32
    stat_left = lax.dot_general(rows, block, (((1,), (1,)), ((), ())), preferred_element_type=f32)
    left_out[0, 0] = decay_rate * left[0, 0] + scale * stat_left
    stat_right = lax.dot_general(columns, block, (((0,), (0,)), ((), ())), preferred_element_type=f32)
    mine = stat_right[:share]
    for i in range(1, shares):
        mine = jnp.where(lax.rem(r, shares) == i, stat_right[i * share:(i + 1) * share], mine)
    right_out[0, 0] = decay_rate * right[0, 0] + scale * mine
    half = jnp.dot(lroot[0, 0], block, preferred_element_type=f32).astype(jnp.bfloat16)
    update_out[0, 0] = jnp.dot(half, rroot[0, 0], preferred_element_type=f32).astype(jnp.bfloat16)


def shards(gradients, left_factor, right_factor, left_root, right_root, owner_table):
    owners = lax.axis_size("fsdp")
    replicas = lax.axis_size("replica")
    ways = replicas // CORES
    strip_rows, total_cols = gradients.shape[1:]
    width = left_factor.shape[-1]
    depth, block_rows, share = left_factor.shape[1:4]
    columns = total_cols // width
    per_block = width // strip_rows
    piece = strip_rows // replicas
    sub = SUB if piece % SUB == 0 else piece
    chunks = depth * (piece // sub)
    hops = max(ways - 1, 1)
    geo = (depth, owners, ways, piece, sub, width, per_block, columns)
    bf16 = jnp.bfloat16
    dma = pltpu.SemaphoreType.DMA
    buffers = [
        (columns, ways * piece, width),
        (hops, columns, piece, width),
        (columns, piece, width),
        (chunks, hops, owners, sub, width),
        (chunks, hops, owners, sub, width),
        (chunks, owners, sub, width),
    ]
    planned = sum(2 * math.prod(shape) for shape in buffers) + 4 * 1024 * 1024
    vmem = [pltpu.VMEM(shape, bf16) for shape in buffers]
    blocks = pl.pallas_call(
        functools.partial(exchange, geo),
        out_shape=jax.ShapeDtypeStruct((depth, owners, replicas, piece, width), bf16),
        in_specs=[pl.BlockSpec(memory_space=pltpu.HBM), pl.BlockSpec(memory_space=pltpu.HBM)],
        out_specs=pl.BlockSpec(memory_space=pl.ANY),
        scratch_shapes=[
            pltpu.SMEM(owner_table.shape, jnp.int32),
            vmem[0],
            vmem[1],
            vmem[2],
            pltpu.SMEM((depth, owners), jnp.int32),
            pltpu.SMEM((depth, owners), jnp.int32),
            vmem[3],
            vmem[4],
            vmem[5],
            dma, dma,
            dma((ways,)), dma((ways,)),
            dma((chunks, ways)), dma((chunks, ways)),
            dma((chunks, owners)), dma((chunks, owners)),
            dma((chunks, ways)), dma((chunks, ways)),
            dma((chunks, ways)), dma((chunks, ways)),
            dma((chunks,)),
        ],
        compiler_params=pltpu.CompilerParams(collective_id=0, has_side_effects=True, vmem_limit_bytes=planned),
    )(pltpu.with_memory_space_constraint(owner_table, pltpu.HBM),
      pltpu.with_memory_space_constraint(gradients, pltpu.HBM))
    blocks = blocks.reshape(depth, block_rows, width, width)

    def at(k, j):
        return (k, j, 0, 0)

    factor = pl.BlockSpec((1, 1, share, width), at)
    square = pl.BlockSpec((1, 1, width, width), at)
    left_new, right_new, update = pl.pallas_call(
        functools.partial(precondition, share),
        grid=(depth, block_rows),
        out_shape=(
            jax.ShapeDtypeStruct(left_factor.shape[1:], jnp.float32),
            jax.ShapeDtypeStruct(left_factor.shape[1:], jnp.float32),
            jax.ShapeDtypeStruct(left_factor.shape[1:], bf16),
        ),
        in_specs=[square, factor, factor, factor, square],
        out_specs=(factor, factor, factor),
        compiler_params=pltpu.CompilerParams(vmem_limit_bytes=16 * 1024 * 1024),
    )(blocks, left_factor[0], right_factor[0],
      pltpu.with_memory_space_constraint(left_root[0], pltpu.HBM), right_root[0])
    return (left_new[None], right_new[None], update[None])


def solution(mesh):
    placed = (
        P("replica", "fsdp", None),
        P("fsdp", None, None, "replica", None),
        P("fsdp", None, None, "replica", None),
        P("fsdp", None, None, "replica", None),
        P("fsdp", None, None, None, None),
        P(),
    )
    factors = P("fsdp", None, None, "replica", None)
    return jax.shard_map(
        shards,
        mesh=mesh,
        in_specs=placed,
        out_specs=(factors, factors, factors),
        check_vma=False,
    )
```

time: 42.9 us -> 40 us (0.932)
  local copies, waits for them, and re-layouts: 3.31 us -> 0.01 us
  Pallas kernels: 38.7 us -> 39.2 us
    unnamed x12 -> x6, local copies, waits for them, and re-layouts: 3.31 us -> 0.01 us
    pallas_call x1, Pallas kernels: 3.47 us -> 4.52 us  [shards(): pl.pallas_call(functools.partial(precondition, share), grid=(depth, block...]
    pallas_call x1, Pallas kernels: 35.2 us -> 34.6 us  [shards(): pl.pallas_call(functools.partial(exchange, geo), out_shape=jax.ShapeDtype...]
where the time goes in v2:
time: 40 us; the launch traced here: 39.9 us
  Pallas kernels  39.2 us (98%)
  between operations  0.69 us (2%)
    pallas_call x1, Pallas kernels, shards(): pl.pallas_call(functools.partial(exchange, geo), out_shape=jax.ShapeDtype...  34.6 us
    pallas_call x1, Pallas kernels, shards(): pl.pallas_call(functools.partial(precondition, share), grid=(depth, block...  4.52 us

profile of v2, /device:TPU:0, one launch (start us, length us, event | category | flops | bytes accessed | tf_op | source)
XLA Modules:
  0.0 39.9 jit_solution(4705322519037403090)
XLA Ops:
  0.6 0.0 copy-start
  0.6 0.0 copy-start.1
  0.7 0.0 copy-start.2
  0.7 34.6 %shard_map.85 = bf16[2,8,4,32,512]{4,3,2,1,0:T(8,128)(2,1)S(1)} custom-call(s32[2,16]{1,0:T(2,128)} %table.1, bf16[1,128,8192]{2,1,0:T(8,128)(2,1)} %grad.1), custom_call_target="tpu_custom_call" | custom-call | tf_op jit(solution)/shard_map/pallas_call | solution.py:226
  35.3 0.0 copy-done
  35.3 0.0 copy-done.1
  35.3 0.0 copy-done.2
  35.3 4.5 %shard_map.86 = (f32[2,2,128,512]{3,2,1,0:T(8,128)}, f32[2,2,128,512]{3,2,1,0:T(8,128)}, bf16[2,2,128,512]{3,2,1,0:T(8,128)(2,1)}) custom-call(bf16[2,2,512,512]{3,2,1,0:T(8,128)(2,1)S(1)} %bitcast.8, f32[2,2,128,512]{3,2,1,0:T(8,128)S(1)} %bitcast.10, f32[2,2,128,512]{3,2,1,0:T(8,128)S(1)} %bitcast.11, bf16[2,2,128,512]{3,2,1,0:T(8,128)(2,1)} %bitcast.12, ...), custom_call_target="tpu_custom_call" | custom-call | tf_op jit(solution)/shard_map/pallas_call | solution.py:259
Async XLA Ops:
  0.6 34.7 %copy-start = (bf16[1,2,2,512,512]{4,3,2,1,0:T(8,128)(2,1)S(1)}, bf16[1,2,2,512,512]{4,3,2,1,0:T(8,128)(2,1)}, u32[]{:S(2)}) copy-start(bf16[1,2,2,512,512]{4,3,2,1,0:T(8,128)(2,1)} %param.10) | copy-start | bytes 6291460
  0.6 34.7 %copy-start.1 = (f32[1,2,2,128,512]{4,3,2,1,0:T(8,128)S(1)}, f32[1,2,2,128,512]{4,3,2,1,0:T(8,128)}, u32[]{:S(2)}) copy-start(f32[1,2,2,128,512]{4,3,2,1,0:T(8,128)} %param.7) | copy-start | bytes 3145732
  0.7 34.7 %copy-start.2 = (f32[1,2,2,128,512]{4,3,2,1,0:T(8,128)S(1)}, f32[1,2,2,128,512]{4,3,2,1,0:T(8,128)}, u32[]{:S(2)}) copy-start(f32[1,2,2,128,512]{4,3,2,1,0:T(8,128)} %param.8) | copy-start | bytes 3145732

commit v3 on v2

--- a/solution.py
+++ b/solution.py
@@ -14,10 +14,45 @@
 SUB = 16
 
 
-def exchange(geo, table, grad, out, owner_of, strip, other, same, cols, live, near_out, near_in, ready,
+def lanes_of(share, r):
+    lanes = max(share, 128)
+    return pl.ds(pl.multiple_of(lax.div(r, lanes // share) * lanes, 128), lanes)
+
+
+def products(share, r, whole, rows, columns, left, right, lroot, rroot):
+    scale = (1.0 - decay_rate) / whole.shape[0]
+    shares = columns.shape[1] // share
+    f32 = jnp.float32
+    stat_left = lax.dot_general(rows, whole, (((1,), (1,)), ((), ())), preferred_element_type=f32)
+    left_new = decay_rate * left[...] + scale * stat_left
+    stat_right = lax.dot_general(columns, whole, (((0,), (0,)), ((), ())), preferred_element_type=f32)
+    mine = stat_right[:share]
+    for i in range(1, shares):
+        mine = jnp.where(lax.rem(r, shares) == i, stat_right[i * share:(i + 1) * share], mine)
+    right_new = decay_rate * right[...] + scale * mine
+    half = jnp.dot(lroot[...], whole, preferred_element_type=f32).astype(jnp.bfloat16)
+    update = jnp.dot(half, rroot[...], preferred_element_type=f32).astype(jnp.bfloat16)
+    return left_new, right_new, update
+
+
+def exchange(geo, table, grad, *refs):
+    (depth, owners, ways, piece, sub, width, per_block, columns, share) = geo
+    early = depth - 1
+    refs = list(refs)
+    given = [refs.pop(0) for _ in range(4)]
+    out, kept = refs.pop(0), refs.pop(0)
+    done = [refs.pop(0) for _ in range(3)] if early else []
+    held = [refs.pop(0) for _ in range(6)] if early else []
+    early_in, early_out, block_sem = (refs.pop(0) for _ in range(3))
+    _exchange(geo, table, grad, given, out, kept, done, held, early_in, early_out, block_sem, *refs)
+
+
+def _exchange(geo, table, grad, given, out, kept, done, held, early_in, early_out, block_sem, owner_of, strip, other, same, cols, live, near_out, near_in, ready,
              table_sem, load_sem, s1, r1, s2, r2, s3, r3, s4, r4, s5, r5, own_sem):
-    depth, owners, ways, piece, sub, width, per_block, columns = geo
-    chunks = [(k, i) for k in range(depth) for i in range(piece // sub)]
+    depth, owners, ways, piece, sub, width, per_block, columns, share = geo
+    early = depth - 1
+    subs = piece // sub
+    chunks = [(k, i) for k in range(depth) for i in range(subs)]
     f = lax.axis_index("fsdp")
     r = lax.axis_index("replica")
     c, y = lax.rem(r, CORES), lax.div(r, CORES)
@@ -59,7 +94,8 @@
         return copy
 
     pairs = {}
-    for step in list(range(1, ways)) + [0]:
+
+    def to_pair(step):
         into = other.at[step - 1] if step else same
         start = pl.multiple_of((1 - c) * half + far_y(step) * piece, 16)
         for col in range(columns):
@@ -68,6 +104,8 @@
         pairs[step] = copy_to(into, into, s1.at[step], r1.at[step], replica=mate)
         pending.append(pairs[step])
 
+    for step in range(1, ways):
+        to_pair(step)
     names.wait()
     row = lax.div(f, per_block)
 
@@ -95,10 +133,10 @@
         theirs = other[step - 1, col, here, :] if step else same[col, here, :]
         return strip[col, pl.ds(low, sub), :].astype(kind) + theirs.astype(kind)
 
-    second = [[] for _ in chunks]
-    for step in range(1, ways):
-        pairs[step].wait_recv()
-    for n in range(len(chunks)):
+    second = {}
+
+    def to_far(n):
+        second[n] = []
         for step in range(1, ways):
             def add(d, carry):
                 near_out[n, step - 1, d] = pair(n, d, step, jnp.bfloat16)
@@ -107,6 +145,18 @@
             lax.fori_loop(0, owners, add, 0)
             second[n].append(send(near_out.at[n, step - 1], near_in.at[n, step - 1], s2.at[n, step], r2.at[n, step],
                                   replica=far_y(step) * CORES + c))
+
+    for step in range(1, ways):
+        pairs[step].wait_recv()
+    to_far(0)
+    to_pair(0)
+    loads = [pltpu.make_async_copy(given[2].at[depth - 1], kept, early_in.at[0])]
+    for i in range(4 if early else 0):
+        loads.append(pltpu.make_async_copy(given[i].at[pl.ds(0, early)], held[i], early_in.at[i + 1]))
+    for load in loads:
+        load.start()
+    if len(chunks) > 1:
+        to_far(1)
     pairs[0].wait_recv()
 
     def rows(n, source):
@@ -151,50 +201,105 @@
                                   replica=far_y(step) * CORES + c))
         fourth[n].append(send(rows(n, r), rows(n, r), s5.at[n, 0], r5.at[n, 0], replica=mate))
 
-    last = []
+    last = {}
 
     def to_mate(n):
-        last.append(fourth[n][-1])
+        last[n] = [fourth[n][-1]]
         for step in range(1, ways):
             fourth[n][step - 1].wait_recv()
             source = lax.rem(y + ways - step, ways) * CORES + c
-            last.append(send(rows(n, source), rows(n, source), s5.at[n, step], r5.at[n, step], replica=mate))
+            last[n].append(send(rows(n, source), rows(n, source), s5.at[n, step], r5.at[n, step], replica=mate))
+
+    def multiply(k):
+        for n in range(k * subs, (k + 1) * subs):
+            for copy in last.pop(n):
+                copy.wait_recv()
+        left, right, lroot, rroot, update, block = held
+        fetch = pltpu.make_async_copy(out.at[k], block.at[k], block_sem.at[k])
+        fetch.start()
+        if k == 0:
+            for load in loads[1:]:
+                load.wait()
+        fetch.wait()
+        for j in range(owners // per_block):
+            strips = pl.ds(j * per_block, per_block)
+            whole = block[k, strips].reshape(width, width)
+            columns_mine = block[k, strips, :, :, lanes_of(share, r)].reshape(width, -1)
+            strip_rows = ways * CORES * piece
+            if share % strip_rows == 0:
+                held_rows = block[k, pl.ds(j * per_block + r * (share // strip_rows), share // strip_rows)]
+            else:
+                first_piece = lax.div(lax.rem(r * share, strip_rows), piece)
+                held_rows = block[k, j * per_block + lax.div(r * share, strip_rows), pl.ds(first_piece, share // piece)]
+            value = products(share, r, whole, held_rows.reshape(share, width), columns_mine,
+                             left.at[k, j], right.at[k, j], lroot.at[k, j], rroot.at[k, j])
+            left[k, j], right[k, j], update[k, j] = value
+        stores = []
+        for i, source in enumerate((left, right, update)):
+            stores.append(pltpu.make_async_copy(source.at[k], done[i].at[k], early_out.at[k, i]))
+            stores[-1].start()
+        return stores
 
     count = len(chunks)
     for n in range(count):
         to_owners(n)
+        if n + 2 < count:
+            to_far(n + 2)
         if n >= 2:
             to_near(n - 2)
+    late = list(range(count))
+    if count > 2:
+        to_mate(late.pop(0))
     for n in range(max(count - 2, 0), count):
         to_near(n)
-        if n >= 2:
-            to_mate(n - 2)
-    for n in range(max(count - 2, 0), count):
+    stores = []
+    for n in late:
         to_mate(n)
-    for copy in last:
-        copy.wait_recv()
+        k = n // subs
+        if k < early and n == (k + 1) * subs - 1:
+            stores += multiply(k)
+    for copies in last.values():
+        for copy in copies:
+            copy.wait_recv()
     for copy in pending:
         copy.wait_send()
-
-
-def precondition(share, whole, left, right, lroot, rroot, left_out, right_out, update_out):
+    loads[0].wait()
+    for store in stores:
+        store.wait()
+
+
+def precondition(early, share, *refs):
+    refs = list(refs)
+    blocks, left, right, lroot, rroot = (refs.pop(0) for _ in range(5))
+    ready = [refs.pop(0) for _ in range(3)] if early else []
+    outs = [refs.pop(0) for _ in range(3)]
+    block, mine, answer = refs.pop(0), [refs.pop(0) for _ in range(4)], refs.pop(0)
+    in_sem, ready_sem, out_sem = refs
     r = lax.axis_index("replica")
-    block = whole[0, 0]
-    scale = (1.0 - decay_rate) / block.shape[0]
-    rows = whole[0, 0, pl.ds(pl.multiple_of(r * share, 16), share), :]
-    lanes = max(share, 128)
-    shares = lanes // share
-    columns = whole[0, 0, :, pl.ds(pl.multiple_of(lax.div(r, shares) * lanes, 128), lanes)]
-    f32 = jnp.float32
-    stat_left = lax.dot_general(rows, block, (((1,), (1,)), ((), ())), preferred_element_type=f32)
-    left_out[0, 0] = decay_rate * left[0, 0] + scale * stat_left
-    stat_right = lax.dot_general(columns, block, (((0,), (0,)), ((), ())), preferred_element_type=f32)
-    mine = stat_right[:share]
-    for i in range(1, shares):
-        mine = jnp.where(lax.rem(r, shares) == i, stat_right[i * share:(i + 1) * share], mine)
-    right_out[0, 0] = decay_rate * right[0, 0] + scale * mine
-    half = jnp.dot(lroot[0, 0], block, preferred_element_type=f32).astype(jnp.bfloat16)
-    update_out[0, 0] = jnp.dot(half, rroot[0, 0], preferred_element_type=f32).astype(jnp.bfloat16)
+    count = block.shape[0]
+    fetches = []
+    for j in range(count):
+        sources = [blocks.at[early, j], left.at[early, j], right.at[early, j], lroot.at[j], rroot.at[early, j]]
+        fetches.append([pltpu.make_async_copy(source, target.at[j], in_sem.at[j, i])
+                        for i, (source, target) in enumerate(zip(sources, [block] + mine))])
+        for fetch in fetches[-1]:
+            fetch.start()
+    stores = []
+    for i, source in enumerate(ready):
+        stores.append(pltpu.make_async_copy(source, outs[i].at[pl.ds(0, early)], ready_sem.at[i]))
+        stores[-1].start()
+    for j in range(count):
+        for fetch in fetches[j]:
+            fetch.wait()
+        rows = block[j, pl.ds(pl.multiple_of(r * share, 16), share), :]
+        values = products(share, r, block[j], rows, block[j, :, lanes_of(share, r)], *(ref.at[j] for ref in mine))
+        targets = (mine[0], mine[1], answer)
+        for i in range(3):
+            targets[i][j] = values[i]
+            stores.append(pltpu.make_async_copy(targets[i].at[j], outs[i].at[early, j], out_sem.at[j, i]))
+            stores[-1].start()
+    for store in stores:
+        store.wait()
 
 
 def shards(gradients, left_factor, right_factor, left_root, right_root, owner_table):
@@ -210,7 +315,8 @@
     sub = SUB if piece % SUB == 0 else piece
     chunks = depth * (piece // sub)
     hops = max(ways - 1, 1)
-    geo = (depth, owners, ways, piece, sub, width, per_block, columns)
+    geo = (depth, owners, ways, piece, sub, width, per_block, columns, share)
+    early = depth - 1
     bf16 = jnp.bfloat16
     dma = pltpu.SemaphoreType.DMA
     buffers = [
@@ -221,14 +327,32 @@
         (chunks, hops, owners, sub, width),
         (chunks, owners, sub, width),
     ]
-    planned = sum(2 * math.prod(shape) for shape in buffers) + 4 * 1024 * 1024
     vmem = [pltpu.VMEM(shape, bf16) for shape in buffers]
-    blocks = pl.pallas_call(
+    f32 = jnp.float32
+
+    def parts(count):
+        return [(count, block_rows, share, width)] * 3 + [(count, block_rows, width, width)]
+
+    held = []
+    if early:
+        shapes = parts(early)
+        held = [pltpu.VMEM(shape, kind) for shape, kind in zip(shapes, (f32, f32, bf16, bf16))]
+        held += [pltpu.VMEM(shapes[0], bf16), pltpu.VMEM((early, owners, replicas, piece, width), bf16)]
+    planned = sum(math.prod(ref.shape) * jnp.dtype(ref.dtype).itemsize for ref in vmem + held) + 6 * 1024 * 1024
+    given = [left_factor[0], right_factor[0], left_root[0], right_root[0]]
+    result = parts(depth)[0]
+    anywhere = pl.BlockSpec(memory_space=pl.ANY)
+    first = [jax.ShapeDtypeStruct((depth, owners, replicas, piece, width), bf16),
+             jax.ShapeDtypeStruct(result[1:], bf16)]
+    if early:
+        first += [jax.ShapeDtypeStruct((early,) + result[1:], kind) for kind in (f32, f32, bf16)]
+    blocks, lroot, *ready = pl.pallas_call(
         functools.partial(exchange, geo),
-        out_shape=jax.ShapeDtypeStruct((depth, owners, replicas, piece, width), bf16),
-        in_specs=[pl.BlockSpec(memory_space=pltpu.HBM), pl.BlockSpec(memory_space=pltpu.HBM)],
-        out_specs=pl.BlockSpec(memory_space=pl.ANY),
-        scratch_shapes=[
+        out_shape=tuple(first),
+        in_specs=[pl.BlockSpec(memory_space=pltpu.HBM)] * 6,
+        out_specs=(anywhere,) * len(first),
+        scratch_shapes=held + [
+            dma((5,)), dma((max(early, 1), 3)), dma((max(early, 1),)),
             pltpu.SMEM(owner_table.shape, jnp.int32),
             vmem[0],
             vmem[1],
@@ -247,29 +371,28 @@
             dma((chunks,)),
         ],
         compiler_params=pltpu.CompilerParams(collective_id=0, has_side_effects=True, vmem_limit_bytes=planned),
-    )(pltpu.with_memory_space_constraint(owner_table, pltpu.HBM),
-      pltpu.with_memory_space_constraint(gradients, pltpu.HBM))
+    )(*(pltpu.with_memory_space_constraint(x, pltpu.HBM) for x in [owner_table, gradients] + given))
     blocks = blocks.reshape(depth, block_rows, width, width)
 
-    def at(k, j):
-        return (k, j, 0, 0)
-
-    factor = pl.BlockSpec((1, 1, share, width), at)
-    square = pl.BlockSpec((1, 1, width, width), at)
-    left_new, right_new, update = pl.pallas_call(
-        functools.partial(precondition, share),
-        grid=(depth, block_rows),
-        out_shape=(
-            jax.ShapeDtypeStruct(left_factor.shape[1:], jnp.float32),
-            jax.ShapeDtypeStruct(left_factor.shape[1:], jnp.float32),
-            jax.ShapeDtypeStruct(left_factor.shape[1:], bf16),
-        ),
-        in_specs=[square, factor, factor, factor, square],
-        out_specs=(factor, factor, factor),
-        compiler_params=pltpu.CompilerParams(vmem_limit_bytes=16 * 1024 * 1024),
-    )(blocks, left_factor[0], right_factor[0],
-      pltpu.with_memory_space_constraint(left_root[0], pltpu.HBM), right_root[0])
-    return (left_new[None], right_new[None], update[None])
+    shapes = parts(1)
+    outs = (jax.ShapeDtypeStruct(result, f32), jax.ShapeDtypeStruct(result, f32), jax.ShapeDtypeStruct(result, bf16))
+    results = pl.pallas_call(
+        functools.partial(precondition, early, share),
+        out_shape=outs,
+        in_specs=[anywhere] * (5 + len(ready)),
+        out_specs=(anywhere,) * 3,
+        scratch_shapes=[
+            pltpu.VMEM((block_rows, width, width), bf16),
+            pltpu.VMEM(shapes[0][1:], f32),
+            pltpu.VMEM(shapes[0][1:], f32),
+            pltpu.VMEM(shapes[0][1:], bf16),
+            pltpu.VMEM(shapes[3][1:], bf16),
+            pltpu.VMEM(shapes[0][1:], bf16),
+            dma((block_rows, 5)), dma((3,)), dma((block_rows, 3)),
+        ],
+        compiler_params=pltpu.CompilerParams(vmem_limit_bytes=20 * 1024 * 1024),
+    )(blocks, given[0], given[1], lroot, given[3], *ready)
+    return tuple(x[None] for x in results)
 
 
 def solution(mesh):

time: 40 us -> 38.3 us (0.957)
  Pallas kernels: 39.2 us -> 37.4 us
    pallas_call x2, Pallas kernels: 39.2 us -> 37.4 us  [the longest x1 34.7 us: shards(): pl.pallas_call(functools.partial(exchange, geo), out_shape=tuple(first),...]
where the time goes in v3:
time: 38.3 us; the launch traced here: 38.1 us
  Pallas kernels  37.4 us (98%)
  between operations  0.69 us (2%)
    pallas_call x1, Pallas kernels, shards(): pl.pallas_call(functools.partial(exchange, geo), out_shape=tuple(first),...  34.7 us
    pallas_call x1, Pallas kernels, shards(): pl.pallas_call(functools.partial(precondition, early, share), out_shape=o...  2.69 us

profile of v3, /device:TPU:0, one launch (start us, length us, event | category | flops | bytes accessed | tf_op | source)
XLA Modules:
  0.0 38.1 jit_solution(12861804811239696530)
XLA Ops:
  0.6 0.0 copy-start
  0.6 0.0 copy-start.1
  0.7 0.0 copy-start.2
  0.7 34.7 %shard_map.85 = (bf16[2,8,4,32,512]{4,3,2,1,0:T(8,128)(2,1)S(1)}, bf16[2,128,512]{2,1,0:T(8,128)(2,1)S(1)}, f32[1,2,128,512]{3,2,1,0:T(8,128)S(1)}, f32[1,2,128,...) custom-call(s32[2,16]{1,0:T(2,128)} %table.1, bf16[1,128,8192]{2,1,0:T(8,128)(2,1)} %grad.1, f32[2,2,128,512]{3,2,1,0:T(8,128)} %bitcast.10, ...), custom_call_target="tpu_custom_call" | custom-call | tf_op jit(solution)/shard_map/pallas_call | solution.py:349
  35.4 0.0 copy-done
  35.4 0.0 copy-done.1
  35.4 0.0 copy-done.2
  35.4 2.7 %shard_map.86 = (f32[2,2,128,512]{3,2,1,0:T(8,128)}, f32[2,2,128,512]{3,2,1,0:T(8,128)}, bf16[2,2,128,512]{3,2,1,0:T(8,128)(2,1)}) custom-call(bf16[2,2,512,512]{3,2,1,0:T(8,128)(2,1)S(1)} %bitcast.14, f32[2,2,128,512]{3,2,1,0:T(8,128)S(1)} %bitcast.11, f32[2,2,128,512]{3,2,1,0:T(8,128)S(1)} %bitcast.13, bf16[2,128,512]{2,1,0:T(8,128)(2,1)S(1)} %get-tuple-element.12.refs_3_, ...), custom_call_target="tpu_custom_call" | custom-call | tf_op jit(solution)/shard_map/pallas_call | solution.py:379
Async XLA Ops:
  0.6 34.8 %copy-start = (bf16[1,2,2,512,512]{4,3,2,1,0:T(8,128)(2,1)S(1)}, bf16[1,2,2,512,512]{4,3,2,1,0:T(8,128)(2,1)}, u32[]{:S(2)}) copy-start(bf16[1,2,2,512,512]{4,3,2,1,0:T(8,128)(2,1)} %param.10) | copy-start | bytes 6291460
  0.6 34.8 %copy-start.1 = (f32[1,2,2,128,512]{4,3,2,1,0:T(8,128)S(1)}, f32[1,2,2,128,512]{4,3,2,1,0:T(8,128)}, u32[]{:S(2)}) copy-start(f32[1,2,2,128,512]{4,3,2,1,0:T(8,128)} %param.7) | copy-start | bytes 3145732
  0.7 34.8 %copy-start.2 = (f32[1,2,2,128,512]{4,3,2,1,0:T(8,128)S(1)}, f32[1,2,2,128,512]{4,3,2,1,0:T(8,128)}, u32[]{:S(2)}) copy-start(f32[1,2,2,128,512]{4,3,2,1,0:T(8,128)} %param.8) | copy-start | bytes 3145732

commit v4 on v3

v4 whole, which is shorter than its diff:
```python
import functools
import math

import jax
import jax.numpy as jnp
from jax import lax
from jax.experimental import pallas as pl
from jax.experimental.pallas import tpu as pltpu
from jax.sharding import PartitionSpec as P

decay_rate = 0.9
MESH = pl.DeviceIdType.MESH
CORES = 2
SUB = 16


def lanes_of(share, r):
    lanes = max(share, 128)
    return pl.ds(pl.multiple_of(lax.div(r, lanes // share) * lanes, 128), lanes)


def products(share, r, whole, rows, columns, left, right, lroot, rroot):
    scale = (1.0 - decay_rate) / whole.shape[0]
    shares = columns.shape[1] // share
    f32 = jnp.float32
    stat_left = lax.dot_general(rows, whole, (((1,), (1,)), ((), ())), preferred_element_type=f32)
    left_new = decay_rate * left[...] + scale * stat_left
    stat_right = lax.dot_general(columns, whole, (((0,), (0,)), ((), ())), preferred_element_type=f32)
    mine = stat_right[:share]
    for i in range(1, shares):
        mine = jnp.where(lax.rem(r, shares) == i, stat_right[i * share:(i + 1) * share], mine)
    right_new = decay_rate * right[...] + scale * mine
    half = jnp.dot(lroot[...], whole, preferred_element_type=f32).astype(jnp.bfloat16)
    update = jnp.dot(half, rroot[...], preferred_element_type=f32).astype(jnp.bfloat16)
    return left_new, right_new, update


def exchange(geo, table, grad, *refs):
    refs = list(refs)
    given = [refs.pop(0) for _ in range(4)]
    out, kept = refs.pop(0), refs.pop(0)
    done = [refs.pop(0) for _ in range(3)] if geo[-1] else []
    held = [refs.pop(0) for _ in range(6)] if geo[-1] else []
    early_in, early_out, block_sem = (refs.pop(0) for _ in range(3))
    _exchange(geo, table, grad, given, out, kept, done, held, early_in, early_out, block_sem, *refs)


def _exchange(geo, table, grad, given, out, kept, done, held, early_in, early_out, block_sem,
              owner_of, strip, other, same, pair_far, pair_same, cols, live, near_out, near_in, ready,
              table_sem, load_sem, s1, r1, s2, r2, s3, r3, s4, r4, s5, r5, own_sem):
    depth, owners, ways, piece, sub, width, per_block, columns, share, early = geo
    subs = piece // sub
    chunks = [(k, i) for k in range(depth) for i in range(subs)]
    f = lax.axis_index("fsdp")
    r = lax.axis_index("replica")
    c, y = lax.rem(r, CORES), lax.div(r, CORES)
    mate = y * CORES + (1 - c)
    half = ways * piece

    def far_y(step):
        return lax.rem(y + step, ways)

    def far_f(step):
        return lax.rem(f + step, owners)

    barrier = pltpu.get_barrier_semaphore()
    pl.semaphore_signal(barrier, inc=1, device_id={"replica": mate}, device_id_type=MESH)
    for step in range(1, ways):
        pl.semaphore_signal(barrier, inc=1, device_id={"replica": far_y(step) * CORES + c}, device_id_type=MESH)
    for step in range(1, owners):
        pl.semaphore_signal(barrier, inc=1, device_id={"fsdp": far_f(step)}, device_id_type=MESH)
    names = pltpu.make_async_copy(table, owner_of, table_sem)
    names.start()
    pl.semaphore_wait(barrier, 1 + (ways - 1) + (owners - 1))

    pending = []

    def copy_to(src, dst, s, t, **to):
        return pltpu.make_async_remote_copy(
            src_ref=src, dst_ref=dst, send_sem=s, recv_sem=t, device_id=to, device_id_type=MESH
        )

    def send(src, dst, s, t, **to):
        copy = copy_to(src, dst, s, t, **to)
        copy.start()
        pending.append(copy)
        return copy

    pairs = {}

    def to_pair(step, i):
        into = other.at[step - 1, pl.ds(i * sub, sub)] if step else same.at[pl.ds(i * sub, sub)]
        start = pl.multiple_of((1 - c) * half + far_y(step) * piece + i * sub, 16)
        pairs[step, i] = send(grad.at[0, pl.ds(start, sub)], into, s1.at[step, i], r1.at[step, i], replica=mate)

    def near_rows(step):
        return pl.ds(pl.multiple_of(far_y(step) * piece, 16), piece)

    mine = {}
    for step in list(range(1, ways)) + [0]:
        for i in range(subs if step else 0):
            to_pair(step, i)
        start = pl.multiple_of(c * half + far_y(step) * piece, 16)
        mine[step] = pltpu.make_async_copy(grad.at[0, pl.ds(start, piece)], strip.at[near_rows(step)], load_sem.at[step])
        mine[step].start()
    names.wait()
    row = lax.div(f, per_block)

    def place(d, carry):
        seen = jnp.int32(0)
        spot = [jnp.int32(0)] * depth
        for col in range(columns):
            hit = owner_of[row, col] == d
            for k in range(depth):
                spot[k] = jnp.where(hit & (seen == k), col, spot[k])
            seen = seen + hit.astype(jnp.int32)
        for k in range(depth):
            cols[k, d] = spot[k]
            live[k, d] = jnp.where(seen > k, 1, 0)
        return carry

    lax.fori_loop(0, owners, place, 0)

    def pair(step, i):
        pairs[step, i].wait_recv()
        low = pl.multiple_of(far_y(step) * piece + i * sub, 16)
        here = pl.ds(i * sub, sub)

        def add(col, carry):
            lanes = pl.ds(pl.multiple_of(col * width, 128), width)
            theirs = other[step - 1, here, lanes] if step else same[here, lanes]
            total = strip[pl.ds(low, sub), lanes].astype(jnp.float32) + theirs.astype(jnp.float32)
            if step:
                pair_far[step - 1, col, here, :] = total.astype(jnp.bfloat16)
            else:
                pair_same[col, here, :] = total
            return carry

        lax.fori_loop(0, columns, add, 0)

    second = {}

    def to_far(n):
        second[n] = []
        k, i = chunks[n]
        for step in range(1, ways):
            if k == 0:
                if i == 0:
                    mine[step].wait()
                pair(step, i)

            def pick(d, carry):
                near_out[n, step - 1, d] = pair_far[step - 1, cols[k, d], i * sub:(i + 1) * sub, :]
                return carry

            lax.fori_loop(0, owners, pick, 0)
            second[n].append(send(near_out.at[n, step - 1], near_in.at[n, step - 1], s2.at[n, step], r2.at[n, step],
                                  replica=far_y(step) * CORES + c))

    to_far(0)
    for i in range(subs):
        to_pair(0, i)
    if len(chunks) > 1:
        to_far(1)
    loads = [pltpu.make_async_copy(given[2].at[early], kept, early_in.at[0])]
    for i in range(4 if early else 0):
        loads.append(pltpu.make_async_copy(given[i].at[pl.ds(0, early)], held[i], early_in.at[i + 1]))
    for load in loads:
        load.start()
    mine[0].wait()
    for i in range(subs):
        pair(0, i)

    block_rows = owners // per_block

    def rows(m, source):
        k, j = m // block_rows, m % block_rows
        spot = lax.rem(source, CORES) * ways + lax.div(source, CORES)
        return out.at[k, pl.ds(j * per_block, per_block), spot]

    def row_of(n, source):
        k, i = chunks[n]
        spot = lax.rem(source, CORES) * ways + lax.div(source, CORES)
        return out.at[k, f, spot, pl.ds(i * sub, sub)]

    third = {}

    def to_owners(n):
        for copy in second[n]:
            copy.wait_recv()
        third[n] = []
        for step in list(range(1, owners)) + [0]:
            d = far_f(step)
            k, i = chunks[n]
            total = pair_same[cols[k, d], i * sub:(i + 1) * sub, :]
            for other_y in range(1, ways):
                total = total + near_in[n, other_y - 1, d].astype(jnp.float32)
            total = total * live[chunks[n][0], d].astype(jnp.float32)
            ready[n, step] = total.astype(jnp.bfloat16)
            if step == 0:
                own = pltpu.make_async_copy(ready.at[n, 0], row_of(n, r), own_sem.at[n])
                own.start()
                third[n].append(own)
            else:
                third[n].append(send(ready.at[n, step], row_of(n, r), s3.at[n, step], r3.at[n, step], fsdp=d))

    fourth = {}

    def to_near(k):
        for n in range(k * subs, (k + 1) * subs):
            third[n][-1].wait()
            for copy in third[n][:-1]:
                copy.wait_recv()
        for m in range(k * block_rows, (k + 1) * block_rows):
            fourth[m] = []
            for step in range(1, ways):
                fourth[m].append(send(rows(m, r), rows(m, r), s4.at[m, step], r4.at[m, step],
                                      replica=far_y(step) * CORES + c))
            fourth[m].append(send(rows(m, r), rows(m, r), s5.at[m, 0], r5.at[m, 0], replica=mate))

    last = {}

    def to_mate(n):
        last[n] = [fourth[n][-1]]
        for step in range(1, ways):
            fourth[n][step - 1].wait_recv()
            source = lax.rem(y + ways - step, ways) * CORES + c
            last[n].append(send(rows(n, source), rows(n, source), s5.at[n, step], r5.at[n, step], replica=mate))

    def multiply(m):
        k, j = m // block_rows, m % block_rows
        for copy in last.pop(m):
            copy.wait_recv()
        left, right, lroot, rroot, update, block = held
        fetch = pltpu.make_async_copy(out.at[k, pl.ds(j * per_block, per_block)], block.at[m], block_sem.at[m])
        fetch.start()
        if m == 0:
            for load in loads[1:]:
                load.wait()
        fetch.wait()
        whole = block[m].reshape(width, width)
        columns_mine = block[m, :, :, :, lanes_of(share, r)].reshape(width, -1)
        strip_rows = ways * CORES * piece
        if share % strip_rows == 0:
            held_rows = block[m, pl.ds(r * (share // strip_rows), share // strip_rows)]
        else:
            first_piece = lax.div(lax.rem(r * share, strip_rows), piece)
            held_rows = block[m, lax.div(r * share, strip_rows), pl.ds(first_piece, share // piece)]
        value = products(share, r, whole, held_rows.reshape(share, width), columns_mine,
                         left.at[m], right.at[m], lroot.at[m], rroot.at[m])
        left[m], right[m], update[m] = value
        for i, source in enumerate((left, right, update)):
            stores.append(pltpu.make_async_copy(source.at[m], done[i].at[m], early_out.at[m, i]))
            stores[-1].start()

    stores = []
    count = len(chunks)
    for n in range(count):
        to_owners(n)
        if n + 2 < count:
            to_far(n + 2)
        if n >= subs and n % subs == 0:
            to_near(n // subs - 1)
    to_near(depth - 1)
    for m in range(early + 1):
        to_mate(m)
        if m < early:
            multiply(m)
    for copies in last.values():
        for copy in copies:
            copy.wait_recv()
    for copy in pending:
        copy.wait_send()
    loads[0].wait()
    for store in stores:
        store.wait()


def precondition(early, share, *refs):
    refs = list(refs)
    blocks, left, right, lroot, rroot = (refs.pop(0) for _ in range(5))
    ready = [refs.pop(0) for _ in range(3)] if early else []
    outs = [refs.pop(0) for _ in range(3)]
    block, mine, answer = refs.pop(0), [refs.pop(0) for _ in range(4)], refs.pop(0)
    in_sem, ready_sem, out_sem = refs
    r = lax.axis_index("replica")
    sources = [blocks.at[early], left.at[early], right.at[early], lroot, rroot.at[early]]
    fetches = [pltpu.make_async_copy(source, target, in_sem.at[i])
               for i, (source, target) in enumerate(zip(sources, [block] + mine))]
    for fetch in fetches:
        fetch.start()
    stores = []
    for i, source in enumerate(ready):
        stores.append(pltpu.make_async_copy(source, outs[i].at[pl.ds(0, early)], ready_sem.at[i]))
        stores[-1].start()
    for fetch in fetches:
        fetch.wait()
    rows = block[pl.ds(pl.multiple_of(r * share, 16), share), :]
    values = products(share, r, block[...], rows, block[:, lanes_of(share, r)], *mine)
    for i, target in enumerate((mine[0], mine[1], answer)):
        target[...] = values[i]
        stores.append(pltpu.make_async_copy(target, outs[i].at[early], out_sem.at[i]))
        stores[-1].start()
    for store in stores:
        store.wait()


def shards(gradients, left_factor, right_factor, left_root, right_root, owner_table):
    owners = lax.axis_size("fsdp")
    replicas = lax.axis_size("replica")
    ways = replicas // CORES
    strip_rows, total_cols = gradients.shape[1:]
    width = left_factor.shape[-1]
    depth, block_rows, share = left_factor.shape[1:4]
    columns = total_cols // width
    per_block = width // strip_rows
    piece = strip_rows // replicas
    sub = SUB if piece % SUB == 0 else piece
    chunks = depth * (piece // sub)
    hops = max(ways - 1, 1)
    total = depth * block_rows
    early = total - 1
    geo = (depth, owners, ways, piece, sub, width, per_block, columns, share, early)
    bf16 = jnp.bfloat16
    dma = pltpu.SemaphoreType.DMA
    vmem = [pltpu.VMEM(shape, kind) for shape, kind in (
        ((ways * piece, total_cols), bf16),
        ((hops, piece, total_cols), bf16),
        ((piece, total_cols), bf16),
        ((hops, columns, piece, width), bf16),
        ((columns, piece, width), jnp.float32),
        ((chunks, hops, owners, sub, width), bf16),
        ((chunks, hops, owners, sub, width), bf16),
        ((chunks, owners, sub, width), bf16),
    )]
    f32 = jnp.float32

    def parts(count):
        return [(count, share, width)] * 3 + [(count, width, width)]

    held = []
    if early:
        shapes = parts(early)
        held = [pltpu.VMEM(shape, kind) for shape, kind in zip(shapes, (f32, f32, bf16, bf16))]
        held += [pltpu.VMEM(shapes[0], bf16), pltpu.VMEM((early, per_block, replicas, piece, width), bf16)]
    planned = sum(math.prod(ref.shape) * jnp.dtype(ref.dtype).itemsize for ref in vmem + held) + 6 * 1024 * 1024
    given = [x.reshape(shape) for x, shape in
             zip((left_factor, right_factor, left_root, right_root), parts(total))]
    result = parts(total)[0]
    anywhere = pl.BlockSpec(memory_space=pl.ANY)
    first = [jax.ShapeDtypeStruct((depth, owners, replicas, piece, width), bf16),
             jax.ShapeDtypeStruct(result[1:], bf16)]
    if early:
        first += [jax.ShapeDtypeStruct((early,) + result[1:], kind) for kind in (f32, f32, bf16)]
    blocks, lroot, *ready = pl.pallas_call(
        functools.partial(exchange, geo),
        out_shape=tuple(first),
        in_specs=[pl.BlockSpec(memory_space=pltpu.HBM)] * 6,
        out_specs=(anywhere,) * len(first),
        scratch_shapes=held + [
            dma((5,)), dma((total, 3)), dma((total,)),
            pltpu.SMEM(owner_table.shape, jnp.int32),
            *vmem[:5],
            pltpu.SMEM((depth, owners), jnp.int32),
            pltpu.SMEM((depth, owners), jnp.int32),
            *vmem[5:],
            dma, dma((ways,)),
            dma((ways, piece // sub)), dma((ways, piece // sub)),
            dma((chunks, ways)), dma((chunks, ways)),
            dma((chunks, owners)), dma((chunks, owners)),
            dma((total, ways)), dma((total, ways)),
            dma((total, ways)), dma((total, ways)),
            dma((chunks,)),
        ],
        compiler_params=pltpu.CompilerParams(collective_id=0, has_side_effects=True, vmem_limit_bytes=planned),
    )(*(pltpu.with_memory_space_constraint(x, pltpu.HBM) for x in [owner_table, gradients] + given))
    blocks = blocks.reshape(total, width, width)

    shapes = parts(1)
    outs = (jax.ShapeDtypeStruct(result, f32), jax.ShapeDtypeStruct(result, f32), jax.ShapeDtypeStruct(result, bf16))
    results = pl.pallas_call(
        functools.partial(precondition, early, share),
        out_shape=outs,
        in_specs=[anywhere] * (5 + len(ready)),
        out_specs=(anywhere,) * 3,
        scratch_shapes=[
            pltpu.VMEM((width, width), bf16),
            pltpu.VMEM(shapes[0][1:], f32),
            pltpu.VMEM(shapes[0][1:], f32),
            pltpu.VMEM(shapes[0][1:], bf16),
            pltpu.VMEM(shapes[3][1:], bf16),
            pltpu.VMEM(shapes[0][1:], bf16),
            dma((5,)), dma((3,)), dma((3,)),
        ],
        compiler_params=pltpu.CompilerParams(vmem_limit_bytes=20 * 1024 * 1024),
    )(blocks, given[0], given[1], lroot, given[3], *ready)
    return tuple(x.reshape(left_factor.shape) for x in results)


def solution(mesh):
    placed = (
        P("replica", "fsdp", None),
        P("fsdp", None, None, "replica", None),
        P("fsdp", None, None, "replica", None),
        P("fsdp", None, None, "replica", None),
        P("fsdp", None, None, None, None),
        P(),
    )
    factors = P("fsdp", None, None, "replica", None)
    return jax.shard_map(
        shards,
        mesh=mesh,
        in_specs=placed,
        out_specs=(factors, factors, factors),
        check_vma=False,
    )
```

time: 38.3 us -> 37.8 us (0.987)
  Pallas kernels: 37.4 us -> 37 us
    pallas_call x1, Pallas kernels: 2.69 us -> 1.86 us  [shards(): pl.pallas_call(functools.partial(precondition, early, share), out_shape=o...]
    pallas_call x1, Pallas kernels: 34.7 us -> 35.1 us  [shards(): pl.pallas_call(functools.partial(exchange, geo), out_shape=tuple(first),...]
where the time goes in v4:
time: 37.8 us; the launch traced here: 37.7 us
  Pallas kernels  37 us (98%)
  between operations  0.69 us (2%)
    pallas_call x1, Pallas kernels, shards(): pl.pallas_call(functools.partial(exchange, geo), out_shape=tuple(first),...  35.1 us
    pallas_call x1, Pallas kernels, shards(): pl.pallas_call(functools.partial(precondition, early, share), out_shape=o...  1.86 us

profile of v4, /device:TPU:0, one launch (start us, length us, event | category | flops | bytes accessed | tf_op | source)
XLA Modules:
  0.0 37.7 jit_solution(15492879239980382123)
XLA Ops:
  0.6 0.0 copy-start
  0.6 0.0 copy-start.1
  0.7 0.0 copy-start.2
  0.7 35.1 %shard_map.85 = (bf16[2,8,4,32,512]{4,3,2,1,0:T(8,128)(2,1)S(1)}, bf16[128,512]{1,0:T(8,128)(2,1)S(1)}, f32[3,128,512]{2,1,0:T(8,128)S(1)}, f32[3,128,512]{2,1,0:T(8,128)S(1)}, bf16[3,128,512]{2,1,0:T(8,128)(2,1)S(1)}) custom-call(s32[2,16]{1,0:T(2,128)} %table.1, bf16[1,128,8192]{2,1,0:T(8,128)(2,1)} %grad.1, f32[4,128,512]{2,1,0:T(8,128)} %bitcast.10, ...), custom_call_target="tpu_custom_call" | custom-call | tf_op jit(solution)/shard_map/pallas_call | solution.py:355
  35.8 0.0 copy-done
  35.8 0.0 copy-done.1
  35.8 0.0 copy-done.2
  35.8 1.9 %shard_map.86 = (f32[4,128,512]{2,1,0:T(8,128)}, f32[4,128,512]{2,1,0:T(8,128)}, bf16[4,128,512]{2,1,0:T(8,128)(2,1)}) custom-call(bf16[4,512,512]{2,1,0:T(8,128)(2,1)S(1)} %bitcast.14, f32[4,128,512]{2,1,0:T(8,128)S(1)} %bitcast.11, f32[4,128,512]{2,1,0:T(8,128)S(1)} %bitcast.13, bf16[128,512]{1,0:T(8,128)(2,1)S(1)} %get-tuple-element.12.refs_3_, ...), custom_call_target="tpu_custom_call" | custom-call | tf_op jit(solution)/shard_map/pallas_call | solution.py:381
Async XLA Ops:
  0.6 35.2 %copy-start = (bf16[1,2,2,512,512]{4,3,2,1,0:T(8,128)(2,1)S(1)}, bf16[1,2,2,512,512]{4,3,2,1,0:T(8,128)(2,1)}, u32[]{:S(2)}) copy-start(bf16[1,2,2,512,512]{4,3,2,1,0:T(8,128)(2,1)} %param.10) | copy-start | bytes 6291460
  0.6 35.2 %copy-start.1 = (f32[1,2,2,128,512]{4,3,2,1,0:T(8,128)S(1)}, f32[1,2,2,128,512]{4,3,2,1,0:T(8,128)}, u32[]{:S(2)}) copy-start(f32[1,2,2,128,512]{4,3,2,1,0:T(8,128)} %param.7) | copy-start | bytes 3145732
  0.7 35.2 %copy-start.2 = (f32[1,2,2,128,512]{4,3,2,1,0:T(8,128)S(1)}, f32[1,2,2,128,512]{4,3,2,1,0:T(8,128)}, u32[]{:S(2)}) copy-start(f32[1,2,2,128,512]{4,3,2,1,0:T(8,128)} %param.8) | copy-start | bytes 3145732

commit v5 on v4

--- a/solution.py
+++ b/solution.py
@@ -61,7 +61,14 @@
         return lax.rem(y + step, ways)
 
     def far_f(step):
-        return lax.rem(f + step, owners)
+        if owners & (owners - 1):
+            return lax.rem(f + step, owners)
+        other_f, bit = f, 1
+        while bit <= step:
+            if step & bit:
+                other_f = other_f + (1 - 2 * lax.rem(lax.div(f, bit), 2)) * bit
+            bit *= 2
+        return other_f
 
     barrier = pltpu.get_barrier_semaphore()
     pl.semaphore_signal(barrier, inc=1, device_id={"replica": mate}, device_id_type=MESH)
@@ -106,17 +113,17 @@
     names.wait()
     row = lax.div(f, per_block)
 
+    names_here = [owner_of[row, col] for col in range(columns)]
+
     def place(d, carry):
-        seen = jnp.int32(0)
-        spot = [jnp.int32(0)] * depth
-        for col in range(columns):
-            hit = owner_of[row, col] == d
-            for k in range(depth):
-                spot[k] = jnp.where(hit & (seen == k), col, spot[k])
-            seen = seen + hit.astype(jnp.int32)
+        code = jnp.int32(0)
+        for col in reversed(range(columns)):
+            code = jnp.where(names_here[col] == d, code * (columns + 1) + (col + 1), code)
         for k in range(depth):
-            cols[k, d] = spot[k]
-            live[k, d] = jnp.where(seen > k, 1, 0)
+            digit = lax.rem(code, columns + 1)
+            code = lax.div(code, columns + 1)
+            cols[k, d] = jnp.maximum(digit - 1, 0)
+            live[k, d] = jnp.minimum(digit, 1)
         return carry
 
     lax.fori_loop(0, owners, place, 0)
@@ -180,16 +187,19 @@
 
     def row_of(n, source):
         k, i = chunks[n]
-        spot = lax.rem(source, CORES) * ways + lax.div(source, CORES)
-        return out.at[k, f, spot, pl.ds(i * sub, sub)]
+        return out.at[k, source, c * ways + y, pl.ds(i * sub, sub)]
+
+    def arrived(n, source):
+        @pl.when(f != source)
+        def wait():
+            copy_to(ready.at[n, 0], row_of(n, source), s3.at[n, 0], r3.at[n, source], fsdp=far_f(1)).wait_recv()
 
     third = {}
 
     def to_owners(n):
         for copy in second[n]:
             copy.wait_recv()
-        third[n] = []
-        for step in list(range(1, owners)) + [0]:
+        for step in reversed(range(owners)):
             d = far_f(step)
             k, i = chunks[n]
             total = pair_same[cols[k, d], i * sub:(i + 1) * sub, :]
@@ -198,21 +208,21 @@
             total = total * live[chunks[n][0], d].astype(jnp.float32)
             ready[n, step] = total.astype(jnp.bfloat16)
             if step == 0:
-                own = pltpu.make_async_copy(ready.at[n, 0], row_of(n, r), own_sem.at[n])
-                own.start()
-                third[n].append(own)
+                third[n] = pltpu.make_async_copy(ready.at[n, 0], row_of(n, f), own_sem.at[n])
+                third[n].start()
             else:
-                third[n].append(send(ready.at[n, step], row_of(n, r), s3.at[n, step], r3.at[n, step], fsdp=d))
+                send(ready.at[n, step], row_of(n, f), s3.at[n, step], r3.at[n, f], fsdp=d)
 
     fourth = {}
 
     def to_near(k):
         for n in range(k * subs, (k + 1) * subs):
-            third[n][-1].wait()
-            for copy in third[n][:-1]:
-                copy.wait_recv()
+            third[n].wait()
         for m in range(k * block_rows, (k + 1) * block_rows):
             fourth[m] = []
+            for n in range(k * subs, (k + 1) * subs):
+                for q in range(per_block):
+                    arrived(n, (m % block_rows) * per_block + q)
             for step in range(1, ways):
                 fourth[m].append(send(rows(m, r), rows(m, r), s4.at[m, step], r4.at[m, step],
                                       replica=far_y(step) * CORES + c))

time: 37.8 us -> 37.9 us (level)
  no operation moved by 1% of the time
where the time goes in v5:
time: 37.9 us; the launch traced here: 37.8 us
  Pallas kernels  37.1 us (98%)
  between operations  0.69 us (2%)
    pallas_call x1, Pallas kernels, shards(): pl.pallas_call(functools.partial(exchange, geo), out_shape=tuple(first),...  35.2 us
    pallas_call x1, Pallas kernels, shards(): pl.pallas_call(functools.partial(precondition, early, share), out_shape=o...  1.86 us

profile of v5, /device:TPU:0, one launch (start us, length us, event | category | flops | bytes accessed | tf_op | source)
XLA Modules:
  0.0 37.8 jit_solution(15274905469751133673)
XLA Ops:
  0.6 0.0 copy-start
  0.6 0.0 copy-start.1
  0.7 0.0 copy-start.2
  0.7 35.2 %shard_map.85 = (bf16[2,8,4,32,512]{4,3,2,1,0:T(8,128)(2,1)S(1)}, bf16[128,512]{1,0:T(8,128)(2,1)S(1)}, f32[3,128,512]{2,1,0:T(8,128)S(1)}, f32[3,128,512]{2,1,0:T(8,128)S(1)}, bf16[3,128,512]{2,1,0:T(8,128)(2,1)S(1)}) custom-call(s32[2,16]{1,0:T(2,128)} %table.1, bf16[1,128,8192]{2,1,0:T(8,128)(2,1)} %grad.1, f32[4,128,512]{2,1,0:T(8,128)} %bitcast.10, ...), custom_call_target="tpu_custom_call" | custom-call | tf_op jit(solution)/shard_map/pallas_call | solution.py:365
  35.9 0.0 copy-done
  35.9 0.0 copy-done.1
  35.9 0.0 copy-done.2
  35.9 1.9 %shard_map.86 = (f32[4,128,512]{2,1,0:T(8,128)}, f32[4,128,512]{2,1,0:T(8,128)}, bf16[4,128,512]{2,1,0:T(8,128)(2,1)}) custom-call(bf16[4,512,512]{2,1,0:T(8,128)(2,1)S(1)} %bitcast.14, f32[4,128,512]{2,1,0:T(8,128)S(1)} %bitcast.11, f32[4,128,512]{2,1,0:T(8,128)S(1)} %bitcast.13, bf16[128,512]{1,0:T(8,128)(2,1)S(1)} %get-tuple-element.12.refs_3_, ...), custom_call_target="tpu_custom_call" | custom-call | tf_op jit(solution)/shard_map/pallas_call | solution.py:391
Async XLA Ops:
  0.6 35.3 %copy-start = (bf16[1,2,2,512,512]{4,3,2,1,0:T(8,128)(2,1)S(1)}, bf16[1,2,2,512,512]{4,3,2,1,0:T(8,128)(2,1)}, u32[]{:S(2)}) copy-start(bf16[1,2,2,512,512]{4,3,2,1,0:T(8,128)(2,1)} %param.10) | copy-start | bytes 6291460
  0.6 35.3 %copy-start.1 = (f32[1,2,2,128,512]{4,3,2,1,0:T(8,128)S(1)}, f32[1,2,2,128,512]{4,3,2,1,0:T(8,128)}, u32[]{:S(2)}) copy-start(f32[1,2,2,128,512]{4,3,2,1,0:T(8,128)} %param.7) | copy-start | bytes 3145732
  0.7 35.3 %copy-start.2 = (f32[1,2,2,128,512]{4,3,2,1,0:T(8,128)S(1)}, f32[1,2,2,128,512]{4,3,2,1,0:T(8,128)}, u32[]{:S(2)}) copy-start(f32[1,2,2,128,512]{4,3,2,1,0:T(8,128)} %param.8) | copy-start | bytes 3145732

commit v6 on v5

--- a/solution.py
+++ b/solution.py
@@ -180,10 +180,10 @@
 
     block_rows = owners // per_block
 
-    def rows(m, source):
-        k, j = m // block_rows, m % block_rows
+    def rows(n, j, source):
+        k, i = chunks[n]
         spot = lax.rem(source, CORES) * ways + lax.div(source, CORES)
-        return out.at[k, pl.ds(j * per_block, per_block), spot]
+        return out.at[k, pl.ds(j * per_block, per_block), spot, pl.ds(i * sub, sub)]
 
     def row_of(n, source):
         k, i = chunks[n]
@@ -215,32 +215,33 @@
 
     fourth = {}
 
-    def to_near(k):
-        for n in range(k * subs, (k + 1) * subs):
-            third[n].wait()
-        for m in range(k * block_rows, (k + 1) * block_rows):
-            fourth[m] = []
-            for n in range(k * subs, (k + 1) * subs):
-                for q in range(per_block):
-                    arrived(n, (m % block_rows) * per_block + q)
+    def to_near(n):
+        third[n].wait()
+        for j in range(block_rows):
+            for q in range(per_block):
+                arrived(n, j * per_block + q)
+            u = n * block_rows + j
+            here = rows(n, j, r)
+            fourth[u] = []
             for step in range(1, ways):
-                fourth[m].append(send(rows(m, r), rows(m, r), s4.at[m, step], r4.at[m, step],
-                                      replica=far_y(step) * CORES + c))
-            fourth[m].append(send(rows(m, r), rows(m, r), s5.at[m, 0], r5.at[m, 0], replica=mate))
+                fourth[u].append(send(here, here, s4.at[u, step], r4.at[u, step], replica=far_y(step) * CORES + c))
+            fourth[u].append(send(here, here, s5.at[u, 0], r5.at[u, 0], replica=mate))
 
     last = {}
 
-    def to_mate(n):
-        last[n] = [fourth[n][-1]]
+    def to_mate(n, j):
+        u = n * block_rows + j
+        last[u] = [fourth[u][-1]]
         for step in range(1, ways):
-            fourth[n][step - 1].wait_recv()
-            source = lax.rem(y + ways - step, ways) * CORES + c
-            last[n].append(send(rows(n, source), rows(n, source), s5.at[n, step], r5.at[n, step], replica=mate))
+            fourth[u][step - 1].wait_recv()
+            there = rows(n, j, lax.rem(y + ways - step, ways) * CORES + c)
+            last[u].append(send(there, there, s5.at[u, step], r5.at[u, step], replica=mate))
 
     def multiply(m):
         k, j = m // block_rows, m % block_rows
-        for copy in last.pop(m):
-            copy.wait_recv()
+        for n in range(k * subs, (k + 1) * subs):
+            for copy in last.pop(n * block_rows + j):
+                copy.wait_recv()
         left, right, lroot, rroot, update, block = held
         fetch = pltpu.make_async_copy(out.at[k, pl.ds(j * per_block, per_block)], block.at[m], block_sem.at[m])
         fetch.start()
@@ -269,13 +270,19 @@
         to_owners(n)
         if n + 2 < count:
             to_far(n + 2)
-        if n >= subs and n % subs == 0:
-            to_near(n // subs - 1)
-    to_near(depth - 1)
-    for m in range(early + 1):
-        to_mate(m)
-        if m < early:
-            multiply(m)
+        if n >= 2:
+            to_near(n - 2)
+    for n in range(count):
+        if n == min(1, count - 1):
+            for late in range(max(count - 2, 0), count):
+                to_near(late)
+        k = n // subs
+        for j in range(block_rows):
+            to_mate(n, j)
+            if j and n % subs == subs - 1:
+                multiply(k * block_rows + j - 1)
+        if n % subs == subs - 1 and (k + 1) * block_rows <= early:
+            multiply((k + 1) * block_rows - 1)
     for copies in last.values():
         for copy in copies:
             copy.wait_recv()
@@ -378,8 +385,8 @@
             dma((ways, piece // sub)), dma((ways, piece // sub)),
             dma((chunks, ways)), dma((chunks, ways)),
             dma((chunks, owners)), dma((chunks, owners)),
-            dma((total, ways)), dma((total, ways)),
-            dma((total, ways)), dma((total, ways)),
+            dma((chunks * block_rows, ways)), dma((chunks * block_rows, ways)),
+            dma((chunks * block_rows, ways)), dma((chunks * block_rows, ways)),
             dma((chunks,)),
         ],
         compiler_params=pltpu.CompilerParams(collective_id=0, has_side_effects=True, vmem_limit_bytes=planned),

time: 37.9 us -> 38.2 us (level)
  no operation moved by 1% of the time
where the time goes in v6:
time: 38.2 us; the launch traced here: 38 us
  Pallas kernels  37.3 us (98%)
  between operations  0.69 us (2%)
    pallas_call x1, Pallas kernels, shards(): pl.pallas_call(functools.partial(exchange, geo), out_shape=tuple(first),...  35.5 us
    pallas_call x1, Pallas kernels, shards(): pl.pallas_call(functools.partial(precondition, early, share), out_shape=o...  1.86 us

profile of v6, /device:TPU:0, one launch (start us, length us, event | category | flops | bytes accessed | tf_op | source)
XLA Modules:
  0.0 38.0 jit_solution(17691848231550906934)
XLA Ops:
  0.6 0.0 copy-start
  0.6 0.0 copy-start.1
  0.7 0.0 copy-start.2
  0.7 35.5 %shard_map.85 = (bf16[2,8,4,32,512]{4,3,2,1,0:T(8,128)(2,1)S(1)}, bf16[128,512]{1,0:T(8,128)(2,1)S(1)}, f32[3,128,512]{2,1,0:T(8,128)S(1)}, f32[3,128,512]{2,1,0:T(8,128)S(1)}, bf16[3,128,512]{2,1,0:T(8,128)(2,1)S(1)}) custom-call(s32[2,16]{1,0:T(2,128)} %table.1, bf16[1,128,8192]{2,1,0:T(8,128)(2,1)} %grad.1, f32[4,128,512]{2,1,0:T(8,128)} %bitcast.10, ...), custom_call_target="tpu_custom_call" | custom-call | tf_op jit(solution)/shard_map/pallas_call | solution.py:372
  36.2 0.0 copy-done
  36.2 0.0 copy-done.1
  36.2 0.0 copy-done.2
  36.2 1.9 %shard_map.86 = (f32[4,128,512]{2,1,0:T(8,128)}, f32[4,128,512]{2,1,0:T(8,128)}, bf16[4,128,512]{2,1,0:T(8,128)(2,1)}) custom-call(bf16[4,512,512]{2,1,0:T(8,128)(2,1)S(1)} %bitcast.14, f32[4,128,512]{2,1,0:T(8,128)S(1)} %bitcast.11, f32[4,128,512]{2,1,0:T(8,128)S(1)} %bitcast.13, bf16[128,512]{1,0:T(8,128)(2,1)S(1)} %get-tuple-element.12.refs_3_, ...), custom_call_target="tpu_custom_call" | custom-call | tf_op jit(solution)/shard_map/pallas_call | solution.py:398
Async XLA Ops:
  0.6 35.5 %copy-start = (bf16[1,2,2,512,512]{4,3,2,1,0:T(8,128)(2,1)S(1)}, bf16[1,2,2,512,512]{4,3,2,1,0:T(8,128)(2,1)}, u32[]{:S(2)}) copy-start(bf16[1,2,2,512,512]{4,3,2,1,0:T(8,128)(2,1)} %param.10) | copy-start | bytes 6291460
  0.6 35.5 %copy-start.1 = (f32[1,2,2,128,512]{4,3,2,1,0:T(8,128)S(1)}, f32[1,2,2,128,512]{4,3,2,1,0:T(8,128)}, u32[]{:S(2)}) copy-start(f32[1,2,2,128,512]{4,3,2,1,0:T(8,128)} %param.7) | copy-start | bytes 3145732
  0.7 35.5 %copy-start.2 = (f32[1,2,2,128,512]{4,3,2,1,0:T(8,128)S(1)}, f32[1,2,2,128,512]{4,3,2,1,0:T(8,128)}, u32[]{:S(2)}) copy-start(f32[1,2,2,128,512]{4,3,2,1,0:T(8,128)} %param.8) | copy-start | bytes 3145732

commit v7 on v6

--- a/solution.py
+++ b/solution.py
@@ -47,7 +47,7 @@
 
 def _exchange(geo, table, grad, given, out, kept, done, held, early_in, early_out, block_sem,
               owner_of, strip, other, same, pair_far, pair_same, cols, live, near_out, near_in, ready,
-              table_sem, load_sem, s1, r1, s2, r2, s3, r3, s4, r4, s5, r5, own_sem):
+              here, table_sem, load_sem, s1, r1, s2, r2, s3, r3, s4, r4, s5, r5, own_sem):
     depth, owners, ways, piece, sub, width, per_block, columns, share, early = geo
     subs = piece // sub
     chunks = [(k, i) for k in range(depth) for i in range(subs)]
@@ -71,14 +71,32 @@
         return other_f
 
     barrier = pltpu.get_barrier_semaphore()
-    pl.semaphore_signal(barrier, inc=1, device_id={"replica": mate}, device_id_type=MESH)
-    for step in range(1, ways):
-        pl.semaphore_signal(barrier, inc=1, device_id={"replica": far_y(step) * CORES + c}, device_id_type=MESH)
-    for step in range(1, owners):
-        pl.semaphore_signal(barrier, inc=1, device_id={"fsdp": far_f(step)}, device_id_type=MESH)
+    met_mate, met_y, met_y_mates, met_owners = (here.at[i] for i in range(4))
+
+    def tell(sem, **to):
+        pl.semaphore_signal(sem, inc=1, device_id=to, device_id_type=MESH)
+
+    @pl.when(c == 1)
+    def side_enters():
+        tell(barrier, replica=mate)
+
+    @pl.when(c == 0)
+    def lead_enters():
+        for step in range(1, ways):
+            tell(barrier, replica=far_y(step) * CORES)
+        pl.semaphore_wait(barrier, ways)
+        tell(met_mate, replica=mate)
+        for step in range(1, ways):
+            tell(met_y, replica=far_y(step) * CORES)
+
+    @pl.when(c == 1)
+    def side_goes_on():
+        pl.semaphore_wait(met_mate, 1)
+        for step in range(1, owners):
+            tell(barrier, fsdp=far_f(step))
+
     names = pltpu.make_async_copy(table, owner_of, table_sem)
     names.start()
-    pl.semaphore_wait(barrier, 1 + (ways - 1) + (owners - 1))
 
     pending = []
 
@@ -110,6 +128,12 @@
         start = pl.multiple_of(c * half + far_y(step) * piece, 16)
         mine[step] = pltpu.make_async_copy(grad.at[0, pl.ds(start, piece)], strip.at[near_rows(step)], load_sem.at[step])
         mine[step].start()
+    @pl.when(c == 0)
+    def lead_knows_y():
+        if ways > 1:
+            pl.semaphore_wait(met_y, ways - 1)
+        tell(met_y_mates, replica=mate)
+
     names.wait()
     row = lax.div(f, per_block)
 
@@ -163,6 +187,10 @@
             lax.fori_loop(0, owners, pick, 0)
             second[n].append(send(near_out.at[n, step - 1], near_in.at[n, step - 1], s2.at[n, step], r2.at[n, step],
                                   replica=far_y(step) * CORES + c))
+
+    @pl.when(c == 1)
+    def side_knows_y():
+        pl.semaphore_wait(met_y_mates, 1)
 
     to_far(0)
     for i in range(subs):
@@ -177,6 +205,15 @@
     mine[0].wait()
     for i in range(subs):
         pair(0, i)
+
+    @pl.when(c == 1)
+    def side_knows_owners():
+        pl.semaphore_wait(barrier, owners - 1)
+        tell(met_owners, replica=mate)
+
+    @pl.when(c == 0)
+    def lead_knows_owners():
+        pl.semaphore_wait(met_owners, 1)
 
     block_rows = owners // per_block
 
@@ -221,11 +258,11 @@
             for q in range(per_block):
                 arrived(n, j * per_block + q)
             u = n * block_rows + j
-            here = rows(n, j, r)
+            mine_now = rows(n, j, r)
             fourth[u] = []
             for step in range(1, ways):
-                fourth[u].append(send(here, here, s4.at[u, step], r4.at[u, step], replica=far_y(step) * CORES + c))
-            fourth[u].append(send(here, here, s5.at[u, 0], r5.at[u, 0], replica=mate))
+                fourth[u].append(send(mine_now, mine_now, s4.at[u, step], r4.at[u, step], replica=far_y(step) * CORES + c))
+            fourth[u].append(send(mine_now, mine_now, s5.at[u, 0], r5.at[u, 0], replica=mate))
 
     last = {}
 
@@ -381,6 +418,7 @@
             pltpu.SMEM((depth, owners), jnp.int32),
             pltpu.SMEM((depth, owners), jnp.int32),
             *vmem[5:],
+            pltpu.SemaphoreType.REGULAR((4,)),
             dma, dma((ways,)),
             dma((ways, piece // sub)), dma((ways, piece // sub)),
             dma((chunks, ways)), dma((chunks, ways)),

time: 38.2 us -> 34.6 us (0.906)
  Pallas kernels: 37.3 us -> 33.6 us
    pallas_call x1, Pallas kernels: 35.5 us -> 31.8 us  [shards(): pl.pallas_call(functools.partial(exchange, geo), out_shape=tuple(first),...]
where the time goes in v7:
time: 34.6 us; the launch traced here: 34.3 us
  Pallas kernels  33.6 us (97%)
  between operations  0.69 us (2%)
    pallas_call x1, Pallas kernels, shards(): pl.pallas_call(functools.partial(exchange, geo), out_shape=tuple(first),...  31.8 us
    pallas_call x1, Pallas kernels, shards(): pl.pallas_call(functools.partial(precondition, early, share), out_shape=o...  1.86 us

profile of v7, /device:TPU:0, one launch (start us, length us, event | category | flops | bytes accessed | tf_op | source)
XLA Modules:
  0.0 34.3 jit_solution(13408889059190192542)
XLA Ops:
  0.6 0.0 copy-start
  0.6 0.0 copy-start.1
  0.7 0.0 copy-start.2
  0.7 31.8 %shard_map.85 = (bf16[2,8,4,32,512]{4,3,2,1,0:T(8,128)(2,1)S(1)}, bf16[128,512]{1,0:T(8,128)(2,1)S(1)}, f32[3,128,512]{2,1,0:T(8,128)S(1)}, f32[3,128,512]{2,1,0:T(8,128)S(1)}, bf16[3,128,512]{2,1,0:T(8,128)(2,1)S(1)}) custom-call(s32[2,16]{1,0:T(2,128)} %table.1, bf16[1,128,8192]{2,1,0:T(8,128)(2,1)} %grad.1, f32[4,128,512]{2,1,0:T(8,128)} %bitcast.10, ...), custom_call_target="tpu_custom_call" | custom-call | tf_op jit(solution)/shard_map/pallas_call | solution.py:409
  32.4 0.0 copy-done
  32.4 0.0 copy-done.1
  32.4 0.0 copy-done.2
  32.5 1.9 %shard_map.86 = (f32[4,128,512]{2,1,0:T(8,128)}, f32[4,128,512]{2,1,0:T(8,128)}, bf16[4,128,512]{2,1,0:T(8,128)(2,1)}) custom-call(bf16[4,512,512]{2,1,0:T(8,128)(2,1)S(1)} %bitcast.14, f32[4,128,512]{2,1,0:T(8,128)S(1)} %bitcast.11, f32[4,128,512]{2,1,0:T(8,128)S(1)} %bitcast.13, bf16[128,512]{1,0:T(8,128)(2,1)S(1)} %get-tuple-element.12.refs_3_, ...), custom_call_target="tpu_custom_call" | custom-call | tf_op jit(solution)/shard_map/pallas_call | solution.py:436
Async XLA Ops:
  0.6 31.8 %copy-start = (bf16[1,2,2,512,512]{4,3,2,1,0:T(8,128)(2,1)S(1)}, bf16[1,2,2,512,512]{4,3,2,1,0:T(8,128)(2,1)}, u32[]{:S(2)}) copy-start(bf16[1,2,2,512,512]{4,3,2,1,0:T(8,128)(2,1)} %param.10) | copy-start | bytes 6291460
  0.6 31.8 %copy-start.1 = (f32[1,2,2,128,512]{4,3,2,1,0:T(8,128)S(1)}, f32[1,2,2,128,512]{4,3,2,1,0:T(8,128)}, u32[]{:S(2)}) copy-start(f32[1,2,2,128,512]{4,3,2,1,0:T(8,128)} %param.7) | copy-start | bytes 3145732
  0.7 31.8 %copy-start.2 = (f32[1,2,2,128,512]{4,3,2,1,0:T(8,128)S(1)}, f32[1,2,2,128,512]{4,3,2,1,0:T(8,128)}, u32[]{:S(2)}) copy-start(f32[1,2,2,128,512]{4,3,2,1,0:T(8,128)} %param.8) | copy-start | bytes 3145732

commit v8 on v7

--- a/solution.py
+++ b/solution.py
@@ -51,6 +51,7 @@
     depth, owners, ways, piece, sub, width, per_block, columns, share, early = geo
     subs = piece // sub
     chunks = [(k, i) for k in range(depth) for i in range(subs)]
+    count = len(chunks)
     f = lax.axis_index("fsdp")
     r = lax.axis_index("replica")
     c, y = lax.rem(r, CORES), lax.div(r, CORES)
@@ -236,6 +237,9 @@
     def to_owners(n):
         for copy in second[n]:
             copy.wait_recv()
+        if n >= 2 and n == count - 1:
+            for early_chunk in range(n - 1):
+                to_near(early_chunk)
         for step in reversed(range(owners)):
             d = far_f(step)
             k, i = chunks[n]
@@ -302,22 +306,19 @@
             stores[-1].start()
 
     stores = []
-    count = len(chunks)
     for n in range(count):
         to_owners(n)
         if n + 2 < count:
             to_far(n + 2)
-        if n >= 2:
-            to_near(n - 2)
     for n in range(count):
         if n == min(1, count - 1):
             for late in range(max(count - 2, 0), count):
                 to_near(late)
         k = n // subs
         for j in range(block_rows):
-            to_mate(n, j)
             if j and n % subs == subs - 1:
                 multiply(k * block_rows + j - 1)
+            to_mate(n, j)
         if n % subs == subs - 1 and (k + 1) * block_rows <= early:
             multiply((k + 1) * block_rows - 1)
     for copies in last.values():

time: 34.6 us -> 37.3 us (1.078)
  Pallas kernels: 33.6 us -> 36.5 us
    pallas_call x1, Pallas kernels: 31.8 us -> 34.6 us  [shards(): pl.pallas_call(functools.partial(exchange, geo), out_shape=tuple(first),...]
where the time goes in v8:
time: 37.3 us; the launch traced here: 37.2 us
  Pallas kernels  36.5 us (98%)
  between operations  0.69 us (2%)
    pallas_call x1, Pallas kernels, shards(): pl.pallas_call(functools.partial(exchange, geo), out_shape=tuple(first),...  34.6 us
    pallas_call x1, Pallas kernels, shards(): pl.pallas_call(functools.partial(precondition, early, share), out_shape=o...  1.86 us

profile of v8, /device:TPU:0, one launch (start us, length us, event | category | flops | bytes accessed | tf_op | source)
XLA Modules:
  0.0 37.2 jit_solution(17579716720121068846)
XLA Ops:
  0.6 0.0 copy-start
  0.6 0.0 copy-start.1
  0.7 0.0 copy-start.2
  0.7 34.6 %shard_map.85 = (bf16[2,8,4,32,512]{4,3,2,1,0:T(8,128)(2,1)S(1)}, bf16[128,512]{1,0:T(8,128)(2,1)S(1)}, f32[3,128,512]{2,1,0:T(8,128)S(1)}, f32[3,128,512]{2,1,0:T(8,128)S(1)}, bf16[3,128,512]{2,1,0:T(8,128)(2,1)S(1)}) custom-call(s32[2,16]{1,0:T(2,128)} %table.1, bf16[1,128,8192]{2,1,0:T(8,128)(2,1)} %grad.1, f32[4,128,512]{2,1,0:T(8,128)} %bitcast.10, ...), custom_call_target="tpu_custom_call" | custom-call | tf_op jit(solution)/shard_map/pallas_call | solution.py:410
  35.3 0.0 copy-done
  35.3 0.0 copy-done.1
  35.3 0.0 copy-done.2
  35.3 1.9 %shard_map.86 = (f32[4,128,512]{2,1,0:T(8,128)}, f32[4,128,512]{2,1,0:T(8,128)}, bf16[4,128,512]{2,1,0:T(8,128)(2,1)}) custom-call(bf16[4,512,512]{2,1,0:T(8,128)(2,1)S(1)} %bitcast.14, f32[4,128,512]{2,1,0:T(8,128)S(1)} %bitcast.11, f32[4,128,512]{2,1,0:T(8,128)S(1)} %bitcast.13, bf16[128,512]{1,0:T(8,128)(2,1)S(1)} %get-tuple-element.12.refs_3_, ...), custom_call_target="tpu_custom_call" | custom-call | tf_op jit(solution)/shard_map/pallas_call | solution.py:437
Async XLA Ops:
  0.6 34.6 %copy-start = (bf16[1,2,2,512,512]{4,3,2,1,0:T(8,128)(2,1)S(1)}, bf16[1,2,2,512,512]{4,3,2,1,0:T(8,128)(2,1)}, u32[]{:S(2)}) copy-start(bf16[1,2,2,512,512]{4,3,2,1,0:T(8,128)(2,1)} %param.10) | copy-start | bytes 6291460
  0.6 34.6 %copy-start.1 = (f32[1,2,2,128,512]{4,3,2,1,0:T(8,128)S(1)}, f32[1,2,2,128,512]{4,3,2,1,0:T(8,128)}, u32[]{:S(2)}) copy-start(f32[1,2,2,128,512]{4,3,2,1,0:T(8,128)} %param.7) | copy-start | bytes 3145732
  0.7 34.6 %copy-start.2 = (f32[1,2,2,128,512]{4,3,2,1,0:T(8,128)S(1)}, f32[1,2,2,128,512]{4,3,2,1,0:T(8,128)}, u32[]{:S(2)}) copy-start(f32[1,2,2,128,512]{4,3,2,1,0:T(8,128)} %param.8) | copy-start | bytes 3145732

commit v9 on v7

--- a/solution.py
+++ b/solution.py
@@ -304,11 +304,11 @@
     stores = []
     count = len(chunks)
     for n in range(count):
+        if n >= 2:
+            to_near(n - 2)
         to_owners(n)
         if n + 2 < count:
             to_far(n + 2)
-        if n >= 2:
-            to_near(n - 2)
     for n in range(count):
         if n == min(1, count - 1):
             for late in range(max(count - 2, 0), count):

time: 34.6 us -> 34.6 us (level)
  no operation moved by 1% of the time
where the time goes in v9:
time: 34.6 us; the launch traced here: 34.3 us
  Pallas kernels  33.6 us (97%)
  between operations  0.69 us (2%)
    pallas_call x1, Pallas kernels, shards(): pl.pallas_call(functools.partial(exchange, geo), out_shape=tuple(first),...  31.8 us
    pallas_call x1, Pallas kernels, shards(): pl.pallas_call(functools.partial(precondition, early, share), out_shape=o...  1.86 us

profile of v9, /device:TPU:0, one launch (start us, length us, event | category | flops | bytes accessed | tf_op | source)
XLA Modules:
  0.0 34.3 jit_solution(4025851079526052218)
XLA Ops:
  0.6 0.0 copy-start
  0.6 0.0 copy-start.1
  0.7 0.0 copy-start.2
  0.7 31.8 %shard_map.85 = (bf16[2,8,4,32,512]{4,3,2,1,0:T(8,128)(2,1)S(1)}, bf16[128,512]{1,0:T(8,128)(2,1)S(1)}, f32[3,128,512]{2,1,0:T(8,128)S(1)}, f32[3,128,512]{2,1,0:T(8,128)S(1)}, bf16[3,128,512]{2,1,0:T(8,128)(2,1)S(1)}) custom-call(s32[2,16]{1,0:T(2,128)} %table.1, bf16[1,128,8192]{2,1,0:T(8,128)(2,1)} %grad.1, f32[4,128,512]{2,1,0:T(8,128)} %bitcast.10, ...), custom_call_target="tpu_custom_call" | custom-call | tf_op jit(solution)/shard_map/pallas_call | solution.py:409
  32.4 0.0 copy-done
  32.4 0.0 copy-done.1
  32.4 0.0 copy-done.2
  32.5 1.9 %shard_map.86 = (f32[4,128,512]{2,1,0:T(8,128)}, f32[4,128,512]{2,1,0:T(8,128)}, bf16[4,128,512]{2,1,0:T(8,128)(2,1)}) custom-call(bf16[4,512,512]{2,1,0:T(8,128)(2,1)S(1)} %bitcast.14, f32[4,128,512]{2,1,0:T(8,128)S(1)} %bitcast.11, f32[4,128,512]{2,1,0:T(8,128)S(1)} %bitcast.13, bf16[128,512]{1,0:T(8,128)(2,1)S(1)} %get-tuple-element.12.refs_3_, ...), custom_call_target="tpu_custom_call" | custom-call | tf_op jit(solution)/shard_map/pallas_call | solution.py:436
Async XLA Ops:
  0.6 31.8 %copy-start = (bf16[1,2,2,512,512]{4,3,2,1,0:T(8,128)(2,1)S(1)}, bf16[1,2,2,512,512]{4,3,2,1,0:T(8,128)(2,1)}, u32[]{:S(2)}) copy-start(bf16[1,2,2,512,512]{4,3,2,1,0:T(8,128)(2,1)} %param.10) | copy-start | bytes 6291460
  0.6 31.8 %copy-start.1 = (f32[1,2,2,128,512]{4,3,2,1,0:T(8,128)S(1)}, f32[1,2,2,128,512]{4,3,2,1,0:T(8,128)}, u32[]{:S(2)}) copy-start(f32[1,2,2,128,512]{4,3,2,1,0:T(8,128)} %param.7) | copy-start | bytes 3145732
  0.7 31.8 %copy-start.2 = (f32[1,2,2,128,512]{4,3,2,1,0:T(8,128)S(1)}, f32[1,2,2,128,512]{4,3,2,1,0:T(8,128)}, u32[]{:S(2)}) copy-start(f32[1,2,2,128,512]{4,3,2,1,0:T(8,128)} %param.8) | copy-start | bytes 3145732
